TPU v7x, 128 devices: a whole 4x4x4 slice. The times are simulated.
128 devices in a mesh: seq: 16 (over y, z_lo, core), tp: 8 (over x, z_hi).
Axes of the slice: x: 4, y: 4, z: 4 (z_hi: 2, z_lo: 2; z = z_hi * 2 + z_lo), core: 2. Of those that a mesh axis runs over, the one named last changes fastest.
Arguments:
- tokens: bfloat16 [16384, 2560], P('seq'), may hold values from -6 to 6
- visible: int32 [16384], P('seq'), may hold values from 0 to 1, as said below
- w_in: bfloat16 [2560, 10240], P(None, 'tp'), may hold values from -0.125 to 0.125
- w_out: bfloat16 [10240, 2560], P('tp'), may hold values from -0.0625 to 0.0625
- w_query: bfloat16 [2560, 2048], P(None, 'tp'), may hold values from -4 to 4
- w_key: bfloat16 [2560, 2048], P(None, 'tp'), may hold values from -1 to 1
- w_value: bfloat16 [2560, 2048], P(None, 'tp'), may hold values from -0.125 to 0.125
- w_proj: bfloat16 [2048, 2560], P('tp'), may hold values from -3 to 3
Outputs:
- mixed: float32 [16384, 2560], P('seq', 'tp')
Inputs may be any that keep to these rules, and one draw needn't show every extreme that they name: Among the 1024 positions of each index of seq at most 768 are visible, and some index has exactly 768; exactly 4096 positions are visible in all.
All inputs are finite; a program needn't handle non-finite values.
Results may differ from a plain program's by a relative error of at most 0.04.
Values may be sent and summed in bfloat16 or wider, within the bound.
A program may use at most 256 MiB of HBM per device.

v0:
```python
import jax
import jax.numpy as jnp
from jax import lax
from jax.sharding import PartitionSpec as P

HEAD_DIM = 128


EPSILON = 1e-05


def norm_rows(values):
    row_mean = jnp.mean(values, axis=-1, keepdims=True)
    centred = values - row_mean
    variance = jnp.mean(centred * centred, axis=-1, keepdims=True)
    return centred * lax.rsqrt(variance + EPSILON)


def shards(tokens, visible, w_in, w_out, w_query, w_key, w_value, w_proj):
    row_count, full_width = tokens.shape
    head_count = w_query.shape[1] // HEAD_DIM
    capacity = 3 * row_count // 4
    tp_index = lax.axis_index("tp")
    tp_count = lax.axis_size("tp")
    part_width = full_width // tp_count
    normed = norm_rows(tokens.astype(jnp.float32)).astype(jnp.bfloat16)
    queries = jnp.dot(normed, w_query, preferred_element_type=jnp.float32).astype(jnp.bfloat16)
    own_cols = lax.dynamic_slice_in_dim(tokens, tp_index * part_width, part_width, 1)
    is_live = visible > 0
    local_rank = jnp.cumsum(visible) - 1
    vis_count = jnp.sum(visible)
    positions = jnp.arange(row_count, dtype=jnp.int32)
    matches = (local_rank[None, :] == jnp.arange(capacity, dtype=jnp.int32)[:, None]) & is_live[
        None, :
    ]
    row_of_rank = jnp.sum(jnp.where(matches, positions[None, :], 0), axis=1)
    enc_in = normed[row_of_rank]
    res_cols = own_cols[row_of_rank]
    live_keys = (jnp.arange(capacity, dtype=jnp.int32) < vis_count).astype(jnp.bfloat16)
    hidden = jax.nn.gelu(jnp.dot(enc_in, w_in, preferred_element_type=jnp.float32)).astype(
        jnp.bfloat16
    )
    partial_value = jnp.dot(hidden, w_out, preferred_element_type=jnp.float32)
    ffn_part = lax.psum_scatter(
        partial_value.astype(jnp.bfloat16), "tp", scatter_dimension=1, tiled=True
    ).astype(jnp.float32)
    encoded_cols = (res_cols.astype(jnp.float32) + ffn_part).astype(jnp.bfloat16)
    encoded = lax.all_gather(encoded_cols, "tp", axis=1, tiled=True)
    key_in = norm_rows(encoded.astype(jnp.float32)).astype(jnp.bfloat16)
    key_rows = jnp.dot(key_in, w_key, preferred_element_type=jnp.float32).astype(jnp.bfloat16)
    value_rows = jnp.dot(key_in, w_value, preferred_element_type=jnp.float32).astype(jnp.bfloat16)
    score_scale = HEAD_DIM ** (-0.5)
    query_heads = queries.reshape(row_count, head_count, HEAD_DIM)
    run_max = jnp.full((head_count, row_count), -1e30, jnp.float32)
    part_keys = lax.all_gather(key_rows, "seq", axis=0, tiled=True).reshape(
        -1, head_count, HEAD_DIM
    )
    part_values = lax.all_gather(value_rows, "seq", axis=0, tiled=True).reshape(
        -1, head_count, HEAD_DIM
    )
    alive = (lax.all_gather(live_keys, "seq", axis=0, tiled=True) > 0)[None, None, :]
    scores = (
        jnp.einsum("qhd,khd->hqk", query_heads, part_keys, preferred_element_type=jnp.float32)
        * score_scale
    )
    scores = jnp.where(alive, scores, -1e30)
    new_max = jnp.maximum(run_max, jnp.max(scores, axis=-1))
    weights = jnp.where(alive, jnp.exp(scores - new_max[:, :, None]), 0.0).astype(jnp.bfloat16)
    new_sum = jnp.sum(weights.astype(jnp.float32), axis=-1)
    new_acc = jnp.einsum("hqk,khd->hqd", weights, part_values, preferred_element_type=jnp.float32)
    attended = (new_acc / new_sum[:, :, None]).astype(jnp.bfloat16)
    attended = jnp.transpose(attended, (1, 0, 2)).reshape(row_count, head_count * HEAD_DIM)
    partial_out = jnp.dot(attended, w_proj, preferred_element_type=jnp.float32)
    owned_sum = lax.psum_scatter(
        partial_out.astype(jnp.bfloat16), "tp", scatter_dimension=1, tiled=True
    ).astype(jnp.float32)
    sum_first, sum_second = lax.psum(
        (jnp.sum(owned_sum, axis=1), jnp.sum(owned_sum * owned_sum, axis=1)), "tp"
    )
    row_mean = sum_first / full_width
    variance = sum_second / full_width - row_mean * row_mean
    normal_out = (owned_sum - row_mean[:, None]) * lax.rsqrt(variance[:, None] + EPSILON)
    return own_cols.astype(jnp.float32) + normal_out


def solution(mesh):
    in_specs = (
        P("seq", None),
        P("seq"),
        P(None, "tp"),
        P("tp", None),
        P(None, "tp"),
        P(None, "tp"),
        P(None, "tp"),
        P("tp", None),
    )
    out_specs = P("seq", "tp")
    return jax.shard_map(shards, mesh=mesh, in_specs=in_specs, out_specs=out_specs, check_vma=False)
```

profile of v0, /device:TPU:0, one launch (start us, length us, event | category | flops | bytes accessed | tf_op | source)
XLA Modules:
  0.0 500.3 jit_solution(12241756715468440414)
XLA Ops:
  6.5 0.8 broadcast_compare_fusion
  7.3 1.0 reduce-window.9
  8.6 0.7 select_reduce_fusion
  9.3 3.7 convert_reduce_fusion.1
  13.0 1.5 fusion.3
  14.5 3.6 fusion.4
  18.1 11.8 %gather_fusion.1 = bf16[768,2560]{1,0:T(8,128)(2,1)} fusion(bf16[1024,2560]{1,0:T(8,128)(2,1)} %fusion.4, s32[1024]{0:T(1024)S(1)} %pad_clamp_fusion), kind=kCustom, calls=%fused_computation.1 | custom fusion | bytes 7867392 | tf_op jit(solution)/shard_map/gather | solution.py:37
  29.9 9.3 %fusion.47 = f32[768,1280]{1,0:T(8,128)S(1)} fusion(bf16[768,2560]{1,0:T(8,128)(2,1)} %gather_fusion.1, bf16[2560,1280]{1,0:T(8,128)(2,1)} %param.10), kind=kOutput, calls=%fused_computation.75 | convolution fusion | flops 5033164800 | bytes 14417920 | tf_op jit(solution)/shard_map/dot_general | solution.py:40
  39.2 12.5 %convolution_convert_fusion.1 = bf16[768,2560]{0,1:T(8,128)(2,1)} fusion(bf16[1280,2560]{1,0:T(8,128)(2,1)} %param.11, f32[768,1280]{1,0:T(8,128)S(1)} %fusion.47), kind=kOutput, calls=%fused_computation.23 | convolution fusion | flops 5043978240 | bytes 14417920 | tf_op jit(solution)/shard_map/dot_general | solution.py:43
  51.7 1.6 constant_dynamic-slice_fusion
  53.3 2.6 gather_fusion
  56.2 82.4 %reduce-scatter.3.cloned.1.call-done = bf16[768,320]{0,1:T(8,128)(2,1)} async-done(((bf16[768,2560]{0,1:T(8,128)(2,1)}), bf16[768,320]{0,1:T(8,128)(2,1)}) %reduce-scatter.3.cloned.1.call-update) | async-done | bytes 491536 | tf_op jit(solution)/shard_map/reduce_scatter | solution.py:44
  138.6 1.9 add_convert_fusion
  140.8 68.4 %all-gather.5.cloned.1.call-done = bf16[768,2560]{0,1:T(8,128)(2,1)} async-done(((bf16[768,320]{0,1:T(8,128)(2,1)}), bf16[768,2560]{0,1:T(8,128)(2,1)}) %all-gather.5.cloned.1.call-update) | async-done | bytes 3932176 | tf_op jit(solution)/shard_map/all_gather | solution.py:48
  209.1 2.9 convert_reduce_fusion.2
  212.4 1.1 fusion.7
  213.5 2.2 fusion.35
  215.8 0.6 reduce_sum.83
  216.4 0.6 fusion.41
  217.1 19.2 %all-gather = bf16[16,1,768]{2,1,0:T(2,128)(2,1)S(1)} all-gather(bf16[1,1,768]{2,1,0:T(2,128)(2,1)S(1)} %reshape.107), channel_id=1, replica_groups=mesh['seq'=16,'tp'=8] {'seq'}, dimensions={0}, use_global_device_ids=true | all-gather | bytes 26112 | tf_op jit(solution)/shard_map/all_gather | solution.py:61
  236.5 4.7 convolution_convert_fusion.2
  241.3 2.1 fusion.38
  243.7 12.5 %all-gather.7.cloned.1.call-done = bf16[12288,256]{1,0:T(8,128)(2,1)} async-done(((bf16[768,256]{1,0:T(8,128)(2,1)}), bf16[12288,256]{1,0:T(8,128)(2,1)}) %all-gather.7.cloned.1.call-update) | async-done | bytes 6291472 | tf_op jit(solution)/shard_map/all_gather | solution.py:55
  256.2 38.6 %fusion = (f32[2,1024]{1,0:T(2,128)S(1)}, f32[2,1024,12288]{2,1,0:T(8,128)}) fusion(pred[12288]{0:T(1024)(128)(4,1)S(1)} %reshape.110, bf16[1024,2,128]{0,2,1:T(8,128)(2,1)S(1)} %bitcast.35, bf16[12288,256]{1,0:T(8,128)(2,1)} %all-gather.7.cloned.1.call-done), kind=kOutput, calls=%fused_computation.5 | convolution fusion | flops 6517946368 | bytes 107499520 | tf_op jit(solution)/shard_map/qhd,khd->hqk/dot_general | solution.py:63
  294.8 32.1 %convert_reduce_fusion = f32[2,1024]{1,0:T(2,128)S(1)} fusion(f32[2,1024]{1,0:T(2,128)S(1)} %broadcast_maximum_fusion, f32[2,1024,12288]{2,1,0:T(8,128)} %get-tuple-element.12, pred[12288]{0:T(1024)(128)(4,1)S(1)} %reshape.110), kind=kLoop, calls=%fused_computation.2 | loop fusion | flops 176158720 | bytes 100691968 | tf_op jit(solution)/shard_map/reduce_sum | solution.py:69
  326.9 8.7 %copy.34 = bf16[12288,256]{0,1:T(8,128)(2,1)} copy(bf16[12288,256]{1,0:T(8,128)(2,1)} %all-gather.9.cloned.1.call-done) | data formatting | bytes 12582912 | tf_op jit(solution)/shard_map/reshape | solution.py:58
  335.6 36.2 %fusion.34 = bf16[1024,2,128]{0,2,1:T(8,128)(2,1)S(1)} fusion(bf16[12288,2,128]{0,2,1:T(8,128)(2,1)} %bitcast.33, f32[1024,2]{0,1:T(2,128)S(1)} %bitcast.37, f32[2,1024,12288]{2,1,0:T(8,128)} %get-tuple-element.12, f32[2,1024]{1,0:T(2,128)S(1)} %broadcast_maximum_fusion, pred[12288]{0:T(1024)(128)(4,1)S(1)} %reshape.110), kind=kOutput, calls=%fused_computation.50 | convolution fusion | flops 6568804352 | bytes 107507712 | tf_op jit(solution)/shard_map/hqk,khd->hqd/dot_general | solution.py:70
  371.8 3.9 convolution_convert_fusion
  376.0 92.7 %reduce-scatter.5.cloned.1.call-done = bf16[1024,320]{0,1:T(8,128)(2,1)} async-done(((bf16[1024,2560]{0,1:T(8,128)(2,1)}), bf16[1024,320]{0,1:T(8,128)(2,1)}) %reduce-scatter.5.cloned.1.call-update) | async-done | bytes 655376 | tf_op jit(solution)/shard_map/reduce_scatter | solution.py:74
  468.7 1.3 convert_reduce_fusion.3
  470.0 21.4 %all-reduce = (f32[1024]{0:T(1024)S(1)}, f32[1024]{0:T(1024)S(1)}) all-reduce(f32[1024]{0:T(1024)S(1)} %get-tuple-element.6, f32[1024]{0:T(1024)S(1)} %get-tuple-element.5), channel_id=1, replica_groups=mesh['seq'=16,'tp'=8] {'tp'}, use_global_device_ids=true, to_apply=%region_15.16 | all-reduce | flops 2048 | bytes 16384 | tf_op jit(solution)/shard_map/psum | solution.py:77
  491.4 2.4 fusion.32
  (42 shorter events, 2.3 us)
Async XLA Ops:
  6.5 365.2 %copy-start = (bf16[256,2560]{1,0:T(8,128)(2,1)S(1)}, bf16[256,2560]{1,0:T(8,128)(2,1)}, u32[]{:S(2)}) copy-start(bf16[256,2560]{1,0:T(8,128)(2,1)} %param.15) | copy-start | bytes 3932164
  6.5 132.0 %reduce-scatter.3.cloned.1.call-start = ((), (), s32[]{:S(2)}) async-start(), calls=%async_computation.2 | async-start | bytes 4423680 | tf_op jit(solution)/shard_map/reduce_scatter | solution.py:44
  8.4 4.6 copy-start.1
  51.7 157.5 %all-gather.5.cloned.1.call-start = ((), (), s32[]{:S(2)}) async-start(), calls=%async_computation.3 | async-start | bytes 4423680 | tf_op jit(solution)/shard_map/all_gather | solution.py:48
  140.5 115.7 %all-gather.7.cloned.1.call-start = ((), (), s32[]{:S(2)}) async-start(), calls=%async_computation.4 | async-start | bytes 6684672 | tf_op jit(solution)/shard_map/all_gather | solution.py:55
  209.1 3.3 copy-start.2
  209.1 4.4 copy-start.5
  213.5 2.3 copy-start.4
  215.7 111.1 %all-gather.9.cloned.1.call-start = ((), (), s32[]{:S(2)}) async-start(), calls=%async_computation.5 | async-start | bytes 6684672 | tf_op jit(solution)/shard_map/all_gather | solution.py:58
  236.5 4.7 copy-start.3
  236.5 4.7 copy-start.6
  243.4 225.3 %reduce-scatter.5.cloned.1.call-start = ((), (), s32[]{:S(2)}) async-start(), calls=%async_computation.6 | async-start | bytes 5898240 | tf_op jit(solution)/shard_map/reduce_scatter | solution.py:74
Sparse Core Ops, SparseCore 0:
  51.8 86.7 reduce-scatter.2
  141.1 67.9 all-gather.4
  215.9 40.3 all-gather.6
  257.9 42.9 all-gather.8
  375.8 92.8 reduce-scatter.4
where the time goes:
time: 501 us; the launch traced here: 500 us
  waiting for transfers between devices  256 us (51%)
  matrix products  109 us (22%)
  other arithmetic  54.4 us (11%)
  blocking collectives  40.6 us (8%)
  local copies, waits for them, and re-layouts  25.8 us (5%)
  between operations  13.3 us (3%)
    reduce_scatter x1, waiting for transfers between devices, shards(): lax.psum_scatter(partial_out.astype(jnp.bfloat16), 'tp', scatter_dimensio...  92.7 us
    reduce_scatter x1, waiting for transfers between devices, shards(): lax.psum_scatter(partial_value.astype(jnp.bfloat16), 'tp', scatter_dimens...  82.4 us
    all_gather x1, waiting for transfers between devices, shards(): encoded = lax.all_gather(encoded_cols, 'tp', axis=1, tiled=True)  68.4 us
    dot_general x1, matrix products, shards(): jnp.einsum('qhd,khd->hqk', query_heads, part_keys, preferred_element_type...  38.6 us
    dot_general x1, matrix products, shards(): jnp.einsum('hqk,khd->hqd', weights, part_values, preferred_element_type=j...  36.2 us
    reduce_sum x1, other arithmetic, shards(): new_sum = jnp.sum(weights.astype(jnp.float32), axis=-1)  32.1 us
    psum x1, blocking collectives, shards(): lax.psum((jnp.sum(owned_sum, axis=1), jnp.sum(owned_sum * owned_sum, axis...  21.4 us
    all_gather x1, blocking collectives, shards(): lax.all_gather(live_keys, 'seq', axis=0, tiled=True) > 0  19.2 us
  transfers between devices with their start and end apart: 5, of which 4 were waited for; matrix products, arithmetic and copies ran while one was open for 17% of the time, Pallas kernels for 0%

commit v1 on v0

v1 whole, which is shorter than its diff:
```python
import functools
import math

import jax
import jax.numpy as jnp
from jax import lax
from jax.experimental import pallas as pl
from jax.experimental.pallas import tpu as pltpu
from jax.sharding import PartitionSpec as P

HEAD_DIM = 128
EPSILON = 1e-05
MESH = pl.DeviceIdType.MESH
F32 = jnp.float32
BF16 = jnp.bfloat16
N_SEQ = 16
N_TP = 8
LAST_PHASE = 9


def norm_rows(values):
    row_mean = jnp.mean(values, axis=-1, keepdims=True)
    centred = values - row_mean
    variance = jnp.mean(centred * centred, axis=-1, keepdims=True)
    return centred * lax.rsqrt(variance + EPSILON)


def dot(a, b):
    return jnp.dot(a, b, preferred_element_type=F32)


def dot_t(a, b):
    return lax.dot_general(a, b, (((1,), (1,)), ((), ())), preferred_element_type=F32)


class Sems:
    def __init__(self, send, recv):
        self.send, self.recv, self.used = send, recv, 0

    def take(self, count):
        first = self.used
        self.used += count
        return first


class RingGather:
    def __init__(self, sems, ring, pair, block, device):
        self.sems, self.ring, self.pair = sems, ring, pair
        self.block, self.device = block, device
        self.base = sems.take(9)
        self.sent = []

    def _copy(self, i, ref, device):
        return pltpu.make_async_remote_copy(
            src_ref=ref,
            dst_ref=ref,
            send_sem=self.sems.send.at[self.base + i],
            recv_sem=self.sems.recv.at[self.base + i],
            device_id=device,
            device_id_type=MESH,
        )

    def _send(self, i, ring, pair, half, to_ring, to_pair):
        copy = self._copy(i, self.block(ring, pair, half), self.device(to_ring, to_pair))
        copy.start()
        self.sent.append(copy)

    def _wait(self, i, ring, pair, half):
        self._copy(i, self.block(ring, pair, half), self.device(self.ring, 1 - self.pair)).wait_recv()

    def start(self):
        r, p = self.ring, self.pair
        self._send(0, r, p, None, r, 1 - p)
        self._send(1, r, p, None, r + 1, p)
        self._send(2, r, p, None, r + 3, p)

    def partner(self):
        r, p = self.ring, self.pair
        self._wait(0, r, 1 - p, None)
        self._send(3, r, 1 - p, None, r + 1, p)
        self._send(4, r, 1 - p, None, r + 3, p)

    def sides(self):
        r, p = self.ring, self.pair
        self._wait(1, r + 3, p, None)
        self._send(5, r + 3, p, 0, r + 1, p)
        self._wait(2, r + 1, p, None)
        self._send(6, r + 1, p, 1, r + 3, p)

    def partner_sides(self):
        r, p = self.ring, self.pair
        self._wait(3, r + 3, 1 - p, None)
        self._send(7, r + 3, 1 - p, 0, r + 1, p)
        self._wait(4, r + 1, 1 - p, None)
        self._send(8, r + 1, 1 - p, 1, r + 3, p)

    def far(self):
        self._wait(5, self.ring + 2, self.pair, 0)
        self._wait(6, self.ring + 2, self.pair, 1)

    def partner_far(self):
        self._wait(7, self.ring + 2, 1 - self.pair, 0)
        self._wait(8, self.ring + 2, 1 - self.pair, 1)

    def drain(self):
        for copy in self.sent:
            copy.wait_send()


class CoreShare:
    def __init__(self, sems, block, core, device):
        self.sems, self.block, self.core, self.device = sems, block, core, device
        self.base = sems.take(8)
        self.sent = []

    def _copy(self, i, ring, pair, core):
        ref = self.block(ring, pair, core)
        return pltpu.make_async_remote_copy(
            src_ref=ref,
            dst_ref=ref,
            send_sem=self.sems.send.at[self.base + i],
            recv_sem=self.sems.recv.at[self.base + i],
            device_id=self.device,
            device_id_type=MESH,
        )

    def send(self, i, ring, pair):
        copy = self._copy(i, ring, pair, self.core)
        copy.start()
        self.sent.append(copy)

    def wait(self, i, ring, pair):
        self._copy(i, ring, pair, 1 - self.core).wait_recv()

    def drain(self):
        for copy in self.sent:
            copy.wait_send()


def kernel(
    vis_tile,
    vis_row,
    tok_hbm,
    w_in_hbm,
    w_out_hbm,
    w_q_hbm,
    w_k_hbm,
    w_v_hbm,
    w_p_hbm,
    out_ref,
    tok,
    w_in,
    w_out,
    w_q,
    w_k,
    w_v,
    w_p,
    counts,
    pick_out,
    pick_in,
    own_rows,
    enc_in,
    hidden,
    part_out,
    part_in,
    key_in,
    kv,
    q_ref,
    top_ref,
    acc_ref,
    att_out,
    att_in,
    proj,
    res_out,
    local_sem,
    send_sem,
    recv_sem,
):
    rows, width = tok.shape
    seq = lax.axis_index("seq")
    tp = lax.axis_index("tp")
    core, z_lo, y = seq % 2, (seq // 2) % 2, seq // 4
    x, z_hi = tp // 2, tp % 2
    sems = Sems(send_sem, recv_sem)
    vis_here = width // N_TP // 10
    vis_here = own_rows.shape[0]
    group = vis_here * N_TP
    half_width = width // 2

    def at_seq(index):
        return {"seq": index, "tp": tp}

    def at_tp(index):
        return {"seq": seq, "tp": index}

    def seq_of(ring, pair, which):
        return ((ring % 4) * 2 + pair) * 2 + which

    def tp_of(ring, pair):
        return (ring % 4) * 2 + pair

    locals_ = []
    for i, (src, dst) in enumerate(
        (
            (tok_hbm, tok),
            (w_q_hbm, w_q),
            (w_in_hbm, w_in),
            (w_out_hbm, w_out),
            (w_k_hbm, w_k),
            (w_v_hbm, w_v),
        )
    ):
        copy = pltpu.make_async_copy(src, dst, local_sem.at[i])
        copy.start()
        locals_.append(copy)
    got_tok, got_q, got_in, got_out, got_k, got_v = locals_
    slice_rows = w_p.shape[1] // N_SEQ
    own_slice = pl.ds(pl.multiple_of(seq * slice_rows, slice_rows), slice_rows)
    got_p = pltpu.make_async_copy(w_p_hbm.at[own_slice], w_p.at[tp, own_slice], local_sem.at[6])
    got_p.start()

    barrier = pltpu.get_barrier_semaphore()

    @pl.loop(1, N_SEQ)
    def _(d):
        pl.semaphore_signal(
            barrier, inc=1, device_id=at_seq((seq + d) % N_SEQ), device_id_type=MESH
        )

    @pl.loop(1, N_TP)
    def _(d):
        pl.semaphore_signal(barrier, inc=1, device_id=at_tp((tp + d) % N_TP), device_id_type=MESH)

    pl.semaphore_wait(barrier, N_SEQ + N_TP - 2)

    def remote(src, dst, index, device):
        return pltpu.make_async_remote_copy(
            src_ref=src,
            dst_ref=dst,
            send_sem=send_sem.at[index],
            recv_sem=recv_sem.at[index],
            device_id=device,
            device_id_type=MESH,
        )

    count_base = sems.take(N_SEQ)

    @pl.loop(1, N_SEQ)
    def _(d):
        remote(
            vis_tile, counts.at[seq], count_base + d, at_seq((seq + d) % N_SEQ)
        ).start()

    counts[pl.ds(seq, 1)] = vis_tile[...][None]

    slice_base = sems.take(N_TP)

    @pl.loop(1, N_TP)
    def _(d):
        remote(
            w_p_hbm.at[own_slice], w_p.at[tp, own_slice], slice_base + d, at_tp((tp + d) % N_TP)
        ).start()

    visible = vis_row[...].astype(F32)
    lower = (
        lax.broadcasted_iota(jnp.int32, (rows, rows), 0)
        <= lax.broadcasted_iota(jnp.int32, (rows, rows), 1)
    ).astype(F32).astype(BF16)
    upto = dot(jnp.broadcast_to(visible, (8, rows)).astype(BF16), lower)[:1]

    @pl.loop(1, N_SEQ)
    def _(d):
        remote(
            vis_tile, counts.at[(seq + N_SEQ - d) % N_SEQ], count_base + d, at_seq((seq + d) % N_SEQ)
        ).wait()

    lane_source = lax.broadcasted_iota(jnp.int32, (1, 256), 1) // 16
    before_me = jnp.zeros((1, 1), F32)
    lane_before = jnp.zeros((1, 256), F32)
    lane_count = jnp.zeros((1, 256), F32)
    for s in range(N_SEQ):
        count = jnp.sum(counts[s].astype(F32), axis=1, keepdims=True)
        count = jnp.sum(count, axis=0, keepdims=True)
        before_me = before_me + jnp.where(seq > s, 1.0, 0.0) * count
        lane_before = lane_before + jnp.where(lane_source > s, count, 0.0)
        lane_count = lane_count + jnp.where(lane_source == s, count, 0.0)

    rank = (before_me + upto - 1.0).astype(jnp.int32)
    code = ((rank >> 3) & 15) * 8 + ((rank >> 7) & 7)
    code = jnp.where((visible > 0.0) & ((rank & 7) == tp), code, -1)
    picks = (lax.broadcasted_iota(jnp.int32, (128, rows), 0) == code).astype(F32).astype(BF16)
    got_tok.wait()
    for h in range(2):
        for c in range(0, half_width, 640):
            rows_of = dot(picks, tok[:, h * half_width + c : h * half_width + c + 640])
            rows_of = rows_of.reshape(16, 8, 640)
            if h == 0:
                proj[:, c : c + 640] = rows_of.reshape(128, 640)
            else:
                first = proj[:, c : c + 640].reshape(16, 8, 640)
                both = jnp.concatenate([first, rows_of], axis=1)
                pick_out[:, c : c + 640] = both.reshape(256, 640).astype(BF16)

    pick_base = sems.take(N_SEQ)

    def pick_rows(index):
        return pl.ds(pl.multiple_of(index * 16, 16), 16)

    @pl.loop(1, N_SEQ)
    def _(d):
        to = (seq + d) % N_SEQ
        remote(
            pick_out.at[pick_rows(to)], pick_in.at[pick_rows(seq)], pick_base + d, at_seq(to)
        ).start()

    pick_in[pick_rows(seq)] = pick_out[pick_rows(seq)]

    query_scale = HEAD_DIM ** (-0.5) * math.log2(math.e)
    got_q.wait()

    def make_queries(first, last):
        @pl.loop(first, last)
        def _(c):
            here = pl.ds(pl.multiple_of(c * 128, 128), 128)
            normed = norm_rows(tok[here].astype(F32)).astype(BF16)
            q_ref[here] = (dot(normed, w_q[...]) * query_scale).astype(BF16)

    make_queries(0, 4)

    @pl.loop(1, N_SEQ)
    def _(d):
        to = (seq + d) % N_SEQ
        source = (seq + N_SEQ - d) % N_SEQ
        remote(
            pick_out.at[pick_rows(to)], pick_in.at[pick_rows(source)], pick_base + d, at_seq(to)
        ).wait()

    slot = lax.broadcasted_iota(jnp.int32, (vis_here, 256), 0)
    lane = lax.broadcasted_iota(jnp.int32, (vis_here, 256), 1)
    wanted = (slot * 128 + seq * 8 + tp).astype(F32)
    live = (wanted >= lane_before) & (wanted < lane_before + lane_count)
    live = live & ((lane & 7) == (slot & 7))
    for h in range(2):
        chosen = (live & (((lane >> 3) & 1) == h)).astype(F32).astype(BF16)
        own_rows[:, h * half_width : (h + 1) * half_width] = dot(chosen, pick_in[...])

    def own_block(ref, ring, pair, half):
        first = tp_of(ring, pair) * vis_here
        if half is None:
            return ref.at[pl.ds(pl.multiple_of(first, vis_here), vis_here)]
        part = vis_here // 2
        return ref.at[pl.ds(pl.multiple_of(first + half * part, part), part)]

    def tp_device(ring, pair):
        return at_tp(tp_of(ring, pair))

    mine = pl.ds(pl.multiple_of(tp * vis_here, vis_here), vis_here)
    enc_in[mine] = norm_rows(own_rows[...]).astype(BF16)
    gather_in = RingGather(sems, x, z_hi, functools.partial(own_block, enc_in), tp_device)
    gather_in.start()

    def slice_block(ring, pair, which, half=None):
        here = pl.ds(
            pl.multiple_of(seq_of(ring, pair, which) * slice_rows, slice_rows), slice_rows
        )
        if half is None:
            return w_p.at[:, here]
        return w_p.at[pl.ds(half * (N_TP // 2), N_TP // 2), here]

    def seq_device(ring, pair):
        return at_seq(seq_of(ring, pair, core))

    other_core = at_seq(seq_of(y, z_lo, 1 - core))
    gather_w = RingGather(
        sems, y, z_lo, lambda ring, pair, half: slice_block(ring, pair, core, half), seq_device
    )
    share_w = CoreShare(sems, slice_block, core, other_core)

    make_queries(4, 6)
    gather_in.partner()
    gather_in.sides()
    gather_in.partner_sides()
    got_p.wait()

    @pl.loop(1, N_TP)
    def _(d):
        remote(
            w_p_hbm.at[own_slice],
            w_p.at[(tp + N_TP - d) % N_TP, own_slice],
            slice_base + d,
            at_tp((tp + d) % N_TP),
        ).wait()

    gather_w.start()
    share_w.send(0, y, z_lo)
    got_in.wait()
    gather_in.far()
    gather_in.partner_far()

    @pl.loop(0, hidden.shape[1] // 256)
    def _(c):
        here = pl.ds(pl.multiple_of(c * 256, 256), 256)
        hidden[:, here] = jax.nn.gelu(dot(enc_in[...], w_in[:, here])).astype(BF16)

    gather_w.partner()
    share_w.send(1, y, 1 - z_lo)
    got_out.wait()
    part_base = sems.take(2 * N_TP)

    def part_rows(index):
        return pl.ds(pl.multiple_of(index * vis_here, vis_here), vis_here)

    def part_copy(h, d, source):
        to = (tp + d) % N_TP
        columns = pl.ds(h * half_width, half_width)
        return remote(
            part_out.at[part_rows(to), columns],
            part_in.at[source, :, columns],
            part_base + h * N_TP + d,
            at_tp(to),
        )

    for h in range(2):

        @pl.loop(0, half_width // 256)
        def _(c, h=h):
            here = pl.ds(pl.multiple_of(h * half_width + c * 256, 256), 256)
            part_out[:, here] = dot(hidden[...], w_out[:, here]).astype(BF16)

        @pl.loop(1, N_TP)
        def _(d, h=h):
            part_copy(h, d, tp).start()

    gather_w.sides()
    share_w.send(2, y + 3, z_lo)
    share_w.send(3, y + 1, z_lo)

    for h in range(2):
        columns = slice(h * half_width, (h + 1) * half_width)
        total = part_out[mine, columns].astype(F32)
        for d in range(1, N_TP):
            source = (tp + N_TP - d) % N_TP
            part_copy(h, d, source).wait()
            total = total + part_in[source, :, columns].astype(F32)
        own_rows[:, columns] = (own_rows[:, columns] + total).astype(BF16).astype(F32)

    key_in[mine] = norm_rows(own_rows[...]).astype(BF16)
    gather_key = RingGather(sems, x, z_hi, functools.partial(own_block, key_in), tp_device)
    gather_key.start()
    make_queries(6, 8)
    gather_key.partner()
    gather_key.sides()
    gather_key.partner_sides()
    gather_w.partner_sides()
    share_w.send(4, y + 3, 1 - z_lo)
    share_w.send(5, y + 1, 1 - z_lo)
    got_k.wait()
    got_v.wait()
    gather_key.far()
    gather_key.partner_far()

    kv_width = w_k.shape[1]
    own = seq_of(y, z_lo, core)
    kv[own, :, :kv_width] = dot(key_in[...], w_k[...]).astype(BF16)
    kv[own, :, kv_width:] = dot(key_in[...], w_v[...]).astype(BF16)

    def kv_block(ring, pair, which, half=None):
        index = seq_of(ring, pair, which)
        if half is None:
            return kv.at[index]
        return kv.at[index, pl.ds(half * (group // 2), group // 2)]

    gather_kv = RingGather(
        sems, y, z_lo, lambda ring, pair, half: kv_block(ring, pair, core, half), seq_device
    )
    share_kv = CoreShare(sems, kv_block, core, other_core)
    gather_kv.start()
    share_kv.send(0, y, z_lo)

    ones = jnp.ones((group, HEAD_DIM), BF16)

    def attend(here, blocks):
        for h in range(2):
            cols = slice(h * HEAD_DIM, (h + 1) * HEAD_DIM)
            v_cols = slice(kv_width + h * HEAD_DIM, kv_width + (h + 1) * HEAD_DIM)
            keys = jnp.concatenate([kv[b, :, cols] for b in blocks], axis=0)
            values = jnp.concatenate(
                [jnp.concatenate([kv[b, :, v_cols], ones], axis=1) for b in blocks], axis=0
            )
            scores = dot_t(q_ref[here, cols], keys)
            old = top_ref[h, here]
            new = jnp.maximum(old, jnp.max(scores, axis=1, keepdims=True))
            shrink = jnp.exp2(old - new)
            weights = jnp.exp2(scores - jnp.concatenate([new] * (2 * len(blocks)), axis=1))
            top_ref[h, here] = new
            acc_ref[h, here] = acc_ref[h, here] * jnp.concatenate([shrink] * 2, axis=1) + dot(
                weights.astype(BF16), values
            )

    top_ref[...] = jnp.full(top_ref.shape, -1e30, F32)
    acc_ref[...] = jnp.zeros(acc_ref.shape, F32)

    def both(ring, pair):
        return [seq_of(ring, pair, core), seq_of(ring, pair, 1 - core)]

    def attend_all(blocks):
        @pl.loop(0, rows // 256)
        def _(c):
            attend(pl.ds(pl.multiple_of(c * 256, 256), 256), blocks)

    gather_kv.partner()
    share_kv.send(1, y, 1 - z_lo)
    share_kv.wait(0, y, z_lo)
    share_kv.wait(1, y, 1 - z_lo)
    attend_all(both(y, z_lo) + both(y, 1 - z_lo))
    gather_kv.sides()
    share_kv.send(2, y + 3, z_lo)
    share_kv.send(3, y + 1, z_lo)
    gather_kv.partner_sides()
    share_kv.send(4, y + 3, 1 - z_lo)
    share_kv.send(5, y + 1, 1 - z_lo)
    gather_w.far()
    share_w.send(6, y + 2, z_lo)
    share_kv.wait(2, y + 3, z_lo)
    share_kv.wait(3, y + 1, z_lo)
    attend_all(both(y + 3, z_lo) + both(y + 1, z_lo))
    gather_kv.far()
    share_kv.send(6, y + 2, z_lo)
    gather_kv.partner_far()
    share_kv.send(7, y + 2, 1 - z_lo)
    share_kv.wait(4, y + 3, 1 - z_lo)
    share_kv.wait(5, y + 1, 1 - z_lo)
    attend_all(both(y + 3, 1 - z_lo) + both(y + 1, 1 - z_lo))
    gather_w.partner_far()
    share_w.send(7, y + 2, 1 - z_lo)
    share_kv.wait(6, y + 2, z_lo)
    share_kv.wait(7, y + 2, 1 - z_lo)

    att_base = sems.take(8)
    last_blocks = both(y + 2, z_lo) + both(y + 2, 1 - z_lo)

    def att_copy(i, b, to, source, of):
        return pltpu.make_async_remote_copy(
            src_ref=att_out.at[to],
            dst_ref=att_in.at[source],
            send_sem=send_sem.at[att_base + i * 2 + b],
            recv_sem=recv_sem.at[att_base + i * 2 + of],
            device_id=at_tp(to),
            device_id_type=MESH,
        )

    @pl.loop(0, 4)
    def _(i):
        ring = (x + 1 + i) % 4
        here = pl.ds(pl.multiple_of(ring * 256, 256), 256)
        attend(here, last_blocks)
        for h in range(2):
            done = acc_ref[h, here]
            done = (done[:, :HEAD_DIM] / done[:, HEAD_DIM:]).astype(BF16)
            cols = slice(h * HEAD_DIM, (h + 1) * HEAD_DIM)
            att_out[pl.ds(tp_of(ring, 0), 2), :, cols] = done.reshape(2, 128, HEAD_DIM)

        @pl.when(i < 3)
        def _():
            for b in range(2):
                att_copy(i, b, tp_of(ring, b), tp, z_hi).start()

    to_pair = tp_of(x, 1 - z_hi)
    att_copy(3, 0, to_pair, tp, 0).start()
    att_in[pl.ds(tp, 1)] = att_out[pl.ds(tp, 1)]

    for i, (ring, pair) in enumerate(
        ((y, z_lo), (y, 1 - z_lo), (y + 3, z_lo), (y + 1, z_lo))
        + ((y + 3, 1 - z_lo), (y + 1, 1 - z_lo), (y + 2, z_lo), (y + 2, 1 - z_lo))
    ):
        share_w.wait(i, ring, pair)

    @pl.loop(0, 3)
    def _(i):
        for b in range(2):
            to = tp_of(x + 1 + i, b)
            source = tp_of(x + 3 - i, b)
            copy = att_copy(i, b, to, source, b)
            copy.wait_send()
            copy.wait_recv()

    att_copy(3, 0, to_pair, to_pair, 0).wait()

    @pl.loop(0, width // 256)
    def _(c):
        here = pl.ds(pl.multiple_of(c * 256, 256), 256)
        total = dot(att_in[0], w_p[0, :, here])
        for t in range(1, N_TP):
            total = total + dot(att_in[t], w_p[t, :, here])
        proj[:, here] = total

    normal = norm_rows(proj[...])
    part = width // N_TP
    res_base = sems.take(N_TP)
    for t in range(N_TP):
        res_out[t] = normal[:, t * part : (t + 1) * part].astype(BF16)

    def res_copy(d, source):
        to = (tp + d) % N_TP
        return remote(res_out.at[to], out_ref.at[source], res_base + d, at_tp(to))

    @pl.loop(1, N_TP)
    def _(d):
        res_copy(d, tp).start()

    keep = pltpu.make_async_copy(res_out.at[tp], out_ref.at[tp], local_sem.at[7])
    keep.start()

    @pl.loop(1, N_TP)
    def _(d):
        res_copy(d, (tp + N_TP - d) % N_TP).wait()

    keep.wait()
    for transfer in (gather_in, gather_w, share_w, gather_key, gather_kv, share_kv):
        transfer.drain()


def shards(tokens, visible, w_in, w_out, w_query, w_key, w_value, w_proj):
    rows, width = tokens.shape
    tp_index = lax.axis_index("tp")
    part = width // N_TP
    vis_here = rows // 32
    group = vis_here * N_TP
    any_spec = pl.BlockSpec(memory_space=pl.ANY)
    vmem_spec = pl.BlockSpec(memory_space=pltpu.VMEM)
    heads = w_query.shape[1]
    visible = (visible > 0).astype(jnp.int32)
    result = pl.pallas_call(
        kernel,
        out_shape=jax.ShapeDtypeStruct((N_TP, rows // N_TP, part), BF16),
        in_specs=[vmem_spec] * 2 + [any_spec] * 7,
        out_specs=any_spec,
        scratch_shapes=[
            pltpu.VMEM(tokens.shape, BF16),
            pltpu.VMEM(w_in.shape, BF16),
            pltpu.VMEM(w_out.shape, BF16),
            pltpu.VMEM(w_query.shape, BF16),
            pltpu.VMEM(w_key.shape, BF16),
            pltpu.VMEM(w_value.shape, BF16),
            pltpu.VMEM((N_TP, *w_proj.shape), BF16),
            pltpu.VMEM((N_SEQ, 8, rows // 8), jnp.int32),
            pltpu.VMEM((16 * N_SEQ, width // 2), BF16),
            pltpu.VMEM((16 * N_SEQ, width // 2), BF16),
            pltpu.VMEM((vis_here, width), F32),
            pltpu.VMEM((group, width), BF16),
            pltpu.VMEM((group, w_in.shape[1]), BF16),
            pltpu.VMEM((group, width), BF16),
            pltpu.VMEM((N_TP, vis_here, width), BF16),
            pltpu.VMEM((group, width), BF16),
            pltpu.VMEM((N_SEQ, group, 2 * heads), BF16),
            pltpu.VMEM((rows, heads), BF16),
            pltpu.VMEM((2, rows, HEAD_DIM), F32),
            pltpu.VMEM((2, rows, 2 * HEAD_DIM), F32),
            pltpu.VMEM((N_TP, rows // N_TP, heads), BF16),
            pltpu.VMEM((N_TP, rows // N_TP, heads), BF16),
            pltpu.VMEM((rows // N_TP, width), F32),
            pltpu.VMEM((N_TP, rows // N_TP, part), BF16),
            pltpu.SemaphoreType.DMA((8,)),
            pltpu.SemaphoreType.DMA((136,)),
            pltpu.SemaphoreType.DMA((136,)),
        ],
        compiler_params=pltpu.CompilerParams(
            collective_id=0, has_side_effects=True, vmem_limit_bytes=60 * 1024 * 1024
        ),
        name="generator_step",
    )(
        visible.reshape(8, rows // 8),
        visible.reshape(1, rows),
        tokens,
        w_in,
        w_out,
        w_query,
        w_key,
        w_value,
        w_proj,
    )
    own_cols = lax.dynamic_slice_in_dim(tokens, tp_index * part, part, 1)
    return own_cols.astype(F32) + result.reshape(rows, part).astype(F32)


def solution(mesh):
    in_specs = (
        P("seq", None),
        P("seq"),
        P(None, "tp"),
        P("tp", None),
        P(None, "tp"),
        P(None, "tp"),
        P(None, "tp"),
        P("tp", None),
    )
    out_specs = P("seq", "tp")
    return jax.shard_map(shards, mesh=mesh, in_specs=in_specs, out_specs=out_specs, check_vma=False)
```

time: 501 us -> 145 us (0.29)
  waiting for transfers between devices: 256 us -> 0 us
  Pallas kernels: 0 us -> 137 us
  matrix products: 109 us -> 0 us
  other arithmetic: 54.4 us -> 3.8 us
  blocking collectives: 40.6 us -> 0 us
  local copies, waits for them, and re-layouts: 25.8 us -> 2.3 us
  between operations: 13.3 us -> 0.03 us
    reduce_scatter x2 -> x0, waiting for transfers between devices: 175 us -> none  [the longest x1 92.7 us: shards(): lax.psum_scatter(partial_out.astype(jnp.bfloat16), 'tp', scatter_dimensio...]
    pallas_call x0 -> x1, Pallas kernels: none -> 137 us  [shards(): pl.pallas_call(kernel, out_shape=jax.ShapeDtypeStruct((N_TP, rows // N_TP...]
    dot_general x8 -> x0, matrix products: 109 us -> none  [the longest x1 38.6 us: shards(): jnp.einsum('qhd,khd->hqk', query_heads, part_keys, preferred_element_type...]
    all_gather x3 -> x0, waiting for transfers between devices: 80.9 us -> none  [the longest x1 68.4 us: shards(): encoded = lax.all_gather(encoded_cols, 'tp', axis=1, tiled=True)]
    reduce_sum x8 -> x0, other arithmetic: 43.8 us -> none  [the longest x1 32.1 us: shards(): new_sum = jnp.sum(weights.astype(jnp.float32), axis=-1)]
    psum x1 -> x0, blocking collectives: 21.4 us -> none  [shards(): lax.psum((jnp.sum(owned_sum, axis=1), jnp.sum(owned_sum * owned_sum, axis...]
    all_gather x1 -> x0, blocking collectives: 19.2 us -> none  [shards(): lax.all_gather(live_keys, 'seq', axis=0, tiled=True) > 0]
    gather x3 -> x0, local copies, waits for them, and re-layouts: 14.7 us -> none  [the longest x1 11.8 us: shards(): enc_in = normed[row_of_rank]]
  transfers between devices with their start and end apart: 5 -> 0, of which waited for: 4 -> 0; matrix products, arithmetic and copies ran while one was open for 17% -> 0% of each run, Pallas kernels for 0% -> 0%
where the time goes in v1:
time: 145 us; the launch traced here: 143 us
  Pallas kernels  137 us (94%)
  other arithmetic  3.8 us (3%)
  local copies, waits for them, and re-layouts  2.3 us (2%)
    pallas_call x1, Pallas kernels, shards(): pl.pallas_call(kernel, out_shape=jax.ShapeDtypeStruct((N_TP, rows // N_TP...  137 us

profile of v1, /device:TPU:0, one launch (start us, length us, event | category | flops | bytes accessed | tf_op | source)
XLA Modules:
  0.0 143.3 jit_solution(8514312001741641874)
XLA Ops:
  0.0 1.3 compare_convert_fusion
  1.3 137.2 %generator_step.1 = bf16[8,128,320]{2,1,0:T(8,128)(2,1)} custom-call(s32[8,128]{1,0:T(8,128)} %get-tuple-element.6.vis_tile, s32[1,1024]{1,0:T(1,128)} %bitcast.6, bf16[1024,2560]{1,0:T(8,128)(2,1)} %tok_hbm.1, bf16[2560,1280]{1,0:T(8,128)(2,1)} %w_in_hbm.1, bf16[1280,2560]{1,0:T(8,128)(2,1)} %w_out_hbm.1, bf16[2560,256]{1,0:T(8,128)(2,1)} %w_q_hbm.1, ...), custom_call_target="tpu_custom_call" | custom-call | tf_op jit(solution)/shard_map/generator_step/pallas_call | solution.py:633
  138.5 1.2 bitcast_convert_fusion
  139.7 0.4 copy.10
  140.2 1.6 %constant_dynamic-slice_fusion = bf16[1024,320]{1,0:T(8,128)(2,1)S(1)} fusion(bf16[1024,2560]{1,0:T(8,128)(2,1)} %tok_hbm.1, s32[]{:T(128)S(6)} %select_n.3), kind=kLoop, calls=%fused_computation.3 | loop fusion | bytes 1310724 | tf_op jit(solution)/shard_map/dynamic_slice | solution.py:682
  141.8 0.3 copy.11
  142.0 1.3 convert_add_fusion

commit v2 on v1

v2 whole, which is shorter than its diff:
```python
import functools
import math

import jax
import jax.numpy as jnp
from jax import lax
from jax.experimental import pallas as pl
from jax.experimental.pallas import tpu as pltpu
from jax.sharding import PartitionSpec as P

HEAD_DIM = 128
EPSILON = 1e-05
MESH = pl.DeviceIdType.MESH
F32 = jnp.float32
BF16 = jnp.bfloat16
N_SEQ = 16
N_TP = 8


def norm_rows(values):
    row_mean = jnp.mean(values, axis=-1, keepdims=True)
    centred = values - row_mean
    variance = jnp.mean(centred * centred, axis=-1, keepdims=True)
    return centred * lax.rsqrt(variance + EPSILON)


def dot(a, b):
    return jnp.dot(a, b, preferred_element_type=F32)


def dot_t(a, b):
    return lax.dot_general(a, b, (((1,), (1,)), ((), ())), preferred_element_type=F32)


class Sems:
    def __init__(self, send, recv):
        self.send, self.recv, self.used = send, recv, 0

    def take(self, count):
        first = self.used
        self.used += count
        return first


class RingGather:
    def __init__(self, sems, ring, pair, block, device):
        self.sems, self.ring, self.pair = sems, ring, pair
        self.block, self.device = block, device
        self.base = sems.take(7)
        self.sent = []

    def _copy(self, i, ring, pair, device):
        ref = self.block(ring, pair)
        return pltpu.make_async_remote_copy(
            src_ref=ref,
            dst_ref=ref,
            send_sem=self.sems.send.at[self.base + i],
            recv_sem=self.sems.recv.at[self.base + i],
            device_id=device,
            device_id_type=MESH,
        )

    def _send(self, i, ring, pair, to_ring, to_pair):
        copy = self._copy(i, ring, pair, self.device(to_ring, to_pair))
        copy.start()
        self.sent.append(copy)

    def _wait(self, i, ring, pair):
        self._copy(i, ring, pair, self.device(self.ring, 1 - self.pair)).wait_recv()

    def start(self):
        r, p = self.ring, self.pair
        self._send(0, r, p, r, 1 - p)
        self._send(1, r, p, r + 1, p)
        self._send(2, r, p, r + 3, p)
        self._send(3, r, p, r + 2, p)

    def partner(self):
        r, p = self.ring, self.pair
        self._wait(0, r, 1 - p)
        self._send(4, r, 1 - p, r + 1, p)
        self._send(5, r, 1 - p, r + 3, p)

    def sides(self):
        self._wait(1, self.ring + 3, self.pair)
        self._wait(2, self.ring + 1, self.pair)

    def far(self):
        r, p = self.ring, self.pair
        self._wait(3, r + 2, p)
        self._send(6, r + 2, p, r, 1 - p)

    def partner_sides(self):
        self._wait(4, self.ring + 3, 1 - self.pair)
        self._wait(5, self.ring + 1, 1 - self.pair)

    def partner_far(self):
        self._wait(6, self.ring + 2, 1 - self.pair)

    def drain(self):
        for copy in self.sent:
            copy.wait_send()


class CoreShare:
    def __init__(self, sems, block, core, device):
        self.sems, self.block, self.core, self.device = sems, block, core, device
        self.base = sems.take(8)
        self.sent = []

    def _copy(self, i, ring, pair, core):
        ref = self.block(ring, pair, core)
        return pltpu.make_async_remote_copy(
            src_ref=ref,
            dst_ref=ref,
            send_sem=self.sems.send.at[self.base + i],
            recv_sem=self.sems.recv.at[self.base + i],
            device_id=self.device,
            device_id_type=MESH,
        )

    def send(self, i, ring, pair):
        copy = self._copy(i, ring, pair, self.core)
        copy.start()
        self.sent.append(copy)

    def wait(self, i, ring, pair):
        self._copy(i, ring, pair, 1 - self.core).wait_recv()

    def drain(self):
        for copy in self.sent:
            copy.wait_send()


def kernel(
    vis_tile,
    vis_row,
    tok_hbm,
    w_in_hbm,
    w_out_hbm,
    w_q_hbm,
    w_k_hbm,
    w_v_hbm,
    w_p_hbm,
    out_ref,
    tok,
    w_in,
    w_out,
    w_q,
    w_k,
    w_v,
    w_p,
    counts,
    pick_out,
    pick_in,
    own_rows,
    enc_in,
    hidden,
    part_out,
    far_in,
    both_out,
    side_in,
    pair_out,
    pair_in,
    key_in,
    kv,
    q_ref,
    top_ref,
    acc_ref,
    att_out,
    att_in,
    proj,
    res_out,
    local_sem,
    send_sem,
    recv_sem,
):
    rows, width = tok.shape
    seq = lax.axis_index("seq")
    tp = lax.axis_index("tp")
    core, z_lo, y = seq % 2, (seq // 2) % 2, seq // 4
    x, z_hi = tp // 2, tp % 2
    sems = Sems(send_sem, recv_sem)
    block_rows = own_rows.shape[0] // 2
    group = block_rows * N_TP
    half_width = width // 2

    def at_seq(index):
        return {"seq": index, "tp": tp}

    def at_tp(index):
        return {"seq": seq, "tp": index}

    def seq_of(ring, pair, which):
        return ((ring % 4) * 2 + pair) * 2 + which

    def tp_of(ring, pair):
        return (ring % 4) * 2 + pair

    slice_rows = w_p.shape[2] // 8

    def slice_of(ring, which):
        return pl.ds(pl.multiple_of(((ring % 4) * 2 + which) * slice_rows, slice_rows), slice_rows)

    own_slice = slice_of(y, core)
    loads = [
        pltpu.make_async_copy(src, dst, local_sem.at[i])
        for i, (src, dst) in enumerate(
            (
                (tok_hbm, tok),
                (w_p_hbm.at[own_slice], w_p.at[z_hi, x, own_slice]),
                (w_q_hbm, w_q),
                (w_in_hbm, w_in),
                (w_out_hbm, w_out),
                (w_k_hbm, w_k),
                (w_v_hbm, w_v),
            )
        )
    ]
    got_tok, got_p, got_q, got_in, got_out, got_k, got_v = loads
    for copy in loads[:2]:
        copy.start()

    barrier = pltpu.get_barrier_semaphore()

    @pl.loop(1, N_SEQ)
    def _(d):
        pl.semaphore_signal(
            barrier, inc=1, device_id=at_seq((seq + d) % N_SEQ), device_id_type=MESH
        )

    @pl.loop(1, N_TP)
    def _(d):
        pl.semaphore_signal(barrier, inc=1, device_id=at_tp((tp + d) % N_TP), device_id_type=MESH)

    visible = vis_row[...].astype(F32)
    lower = (
        lax.broadcasted_iota(jnp.int32, (rows, rows), 0)
        <= lax.broadcasted_iota(jnp.int32, (rows, rows), 1)
    ).astype(F32).astype(BF16)
    upto = dot(jnp.broadcast_to(visible, (8, rows)).astype(BF16), lower)[:1]

    pl.semaphore_wait(barrier, N_SEQ + N_TP - 2)

    def remote(src, dst, index, device):
        return pltpu.make_async_remote_copy(
            src_ref=src,
            dst_ref=dst,
            send_sem=send_sem.at[index],
            recv_sem=recv_sem.at[index],
            device_id=device,
            device_id_type=MESH,
        )

    count_base = sems.take(N_SEQ)

    @pl.loop(1, N_SEQ)
    def _(d):
        remote(
            vis_tile, counts.at[seq], count_base + d, at_seq((seq + d) % N_SEQ)
        ).start()

    counts[pl.ds(seq, 1)] = vis_tile[...][None]

    slice_base = sems.take(8)
    pair_device = at_tp(tp_of(x, 1 - z_hi))
    remote(
        w_p_hbm.at[own_slice], w_p.at[z_hi, x, own_slice], slice_base, pair_device
    ).start()

    def slice_copy(of, d, ring):
        here = w_p.at[of, ring, own_slice]
        src = w_p_hbm.at[own_slice] if of is z_hi else w_p.at[of, x, own_slice]
        index = slice_base + d + (0 if of is z_hi else 4)
        return remote(src, here, index, at_tp(tp_of(x + d, z_hi)))

    @pl.loop(1, 4)
    def _(d):
        slice_copy(z_hi, d, x).start()

    @pl.loop(1, N_SEQ)
    def _(d):
        remote(
            vis_tile, counts.at[(seq + N_SEQ - d) % N_SEQ], count_base + d, at_seq((seq + d) % N_SEQ)
        ).wait()

    lane_source = lax.broadcasted_iota(jnp.int32, (1, 256), 1) // 16
    before_me = jnp.zeros((1, 1), F32)
    lane_before = jnp.zeros((1, 256), F32)
    lane_count = jnp.zeros((1, 256), F32)
    for s in range(N_SEQ):
        count = jnp.sum(counts[s].astype(F32), axis=1, keepdims=True)
        count = jnp.sum(count, axis=0, keepdims=True)
        before_me = before_me + jnp.where(seq > s, 1.0, 0.0) * count
        lane_before = lane_before + jnp.where(lane_source > s, count, 0.0)
        lane_count = lane_count + jnp.where(lane_source == s, count, 0.0)

    rank = (before_me + upto - 1.0).astype(jnp.int32)
    code = ((rank >> 3) & 15) * 8 + ((rank >> 7) & 7)
    code = jnp.where((visible > 0.0) & ((rank & 7) == tp), code, -1)
    picks = (lax.broadcasted_iota(jnp.int32, (128, rows), 0) == code).astype(F32).astype(BF16)
    got_tok.wait()
    for h in range(2):
        for c in range(0, half_width, 640):
            rows_of = dot(picks, tok[:, h * half_width + c : h * half_width + c + 640])
            rows_of = rows_of.reshape(16, 8, 640)
            if h == 0:
                proj[:, c : c + 640] = rows_of.reshape(128, 640)
            else:
                first = proj[:, c : c + 640].reshape(16, 8, 640)
                both = jnp.concatenate([first, rows_of], axis=1)
                pick_out[:, c : c + 640] = both.reshape(256, 640).astype(BF16)

    pick_base = sems.take(N_SEQ)

    def pick_rows(index):
        return pl.ds(pl.multiple_of(index * 16, 16), 16)

    @pl.loop(1, N_SEQ)
    def _(d):
        to = (seq + d) % N_SEQ
        remote(
            pick_out.at[pick_rows(to)], pick_in.at[pick_rows(seq)], pick_base + d, at_seq(to)
        ).start()

    pick_in[pick_rows(seq)] = pick_out[pick_rows(seq)]
    other_z = 1 - z_hi
    remote(
        w_p_hbm.at[own_slice], w_p.at[other_z, x, own_slice], slice_base, pair_device
    ).wait()

    @pl.loop(1, 4)
    def _(d):
        slice_copy(other_z, d, x).start()

    for copy in loads[2:]:
        copy.start()

    query_scale = HEAD_DIM ** (-0.5) * math.log2(math.e)
    got_q.wait()

    def make_queries(first, last):
        @pl.loop(first, last)
        def _(c):
            here = pl.ds(pl.multiple_of(c * 128, 128), 128)
            normed = norm_rows(tok[here].astype(F32)).astype(BF16)
            q_ref[here] = (dot(normed, w_q[...]) * query_scale).astype(BF16)

    make_queries(0, 4)

    @pl.loop(1, N_SEQ)
    def _(d):
        to = (seq + d) % N_SEQ
        source = (seq + N_SEQ - d) % N_SEQ
        remote(
            pick_out.at[pick_rows(to)], pick_in.at[pick_rows(source)], pick_base + d, at_seq(to)
        ).wait()

    slot = lax.broadcasted_iota(jnp.int32, (2 * block_rows, 256), 0)
    lane = lax.broadcasted_iota(jnp.int32, (2 * block_rows, 256), 1)
    wanted = (slot * 128 + seq * 8 + tp).astype(F32)
    live = (wanted >= lane_before) & (wanted < lane_before + lane_count)
    live = live & ((lane & 7) == (slot & 7))
    for h in range(2):
        chosen = (live & (((lane >> 3) & 1) == h)).astype(F32).astype(BF16)
        own_rows[:, h * half_width : (h + 1) * half_width] = dot(chosen, pick_in[...])

    def own_block(ref, a, ring, pair):
        first = tp_of(ring, pair) * block_rows
        return ref.at[a, pl.ds(pl.multiple_of(first, block_rows), block_rows)]

    def tp_device(ring, pair):
        return at_tp(tp_of(ring, pair))

    mine = pl.ds(pl.multiple_of(tp * block_rows, block_rows), block_rows)
    halves = [slice(a * block_rows, (a + 1) * block_rows) for a in range(2)]
    gather_in = []
    for a in range(2):
        enc_in[a, mine] = norm_rows(own_rows[halves[a]]).astype(BF16)
        gather_in.append(
            RingGather(sems, x, z_hi, functools.partial(own_block, enc_in, a), tp_device)
        )
        gather_in[a].start()

    def w_block(ring, which, half=None):
        if half is None:
            return w_p.at[:, :, slice_of(ring, which)]
        return w_p.at[half, :, slice_of(ring, which)]

    def seq_device(ring, pair):
        return at_seq(seq_of(ring, pair, core))

    other_core = at_seq(seq_of(y, z_lo, 1 - core))
    up, down = seq_device(y + 1, z_lo), seq_device(y + 3, z_lo)
    w_base = sems.take(8)

    def w_copy(i, ring, which=None, half=None):
        ref = w_block(ring, core if which is None else which, half)
        return remote(ref, ref, w_base + i, (up, down, up, down)[i] if i < 4 else other_core)

    def w_start():
        got_p.wait()

        @pl.loop(1, 4)
        def _(d):
            slice_copy(z_hi, d, (x + 4 - d) % 4).wait()

        @pl.loop(1, 4)
        def _(d):
            slice_copy(other_z, d, (x + 4 - d) % 4).wait()

        w_copy(0, y).start()
        w_copy(1, y).start()
        w_copy(4, y).start()

    def w_sides():
        w_copy(0, y + 3).wait_recv()
        w_copy(2, y + 3, half=0).start()
        w_copy(5, y + 3).start()
        w_copy(1, y + 1).wait_recv()
        w_copy(3, y + 1, half=1).start()
        w_copy(6, y + 1).start()

    def w_far():
        w_copy(2, y + 2, half=0).wait_recv()
        w_copy(3, y + 2, half=1).wait_recv()
        w_copy(7, y + 2).start()
        for i, ring in enumerate((y, y + 3, y + 1, y + 2)):
            w_copy(4 + i, ring, 1 - core).wait_recv()

    def w_drain():
        for i, ring in enumerate((y, y, y + 3, y + 1, y, y + 3, y + 1, y + 2)):
            w_copy(i, ring, half=(None, None, 0, 1)[i] if i < 4 else None).wait_send()

    def to_hidden(a):
        @pl.loop(0, hidden.shape[2] // 256)
        def _(c):
            here = pl.ds(pl.multiple_of(c * 256, 256), 256)
            hidden[a, :, here] = jax.nn.gelu(dot(enc_in[a], w_in[:, here])).astype(BF16)

    def to_part(a):
        @pl.loop(0, width // 256)
        def _(c):
            here = pl.ds(pl.multiple_of(c * 256, 256), 256)
            part_out[a, :, here] = dot(hidden[a], w_out[:, here]).astype(BF16)

    slab_rows = 2 * block_rows
    low, high = pl.ds(0, half_width), pl.ds(half_width, half_width)
    sum_base = [sems.take(7), sems.take(7)]
    right, left = at_tp(tp_of(x + 1, z_hi)), at_tp(tp_of(x + 3, z_hi))

    def slab(ring):
        return pl.ds(pl.multiple_of((ring % 4) * slab_rows, slab_rows), slab_rows)

    def of_pair(pair):
        return pl.ds(pl.multiple_of(pair * block_rows, block_rows), block_rows)

    def of_both(pair):
        first = (x * 2 + pair) * block_rows
        return pl.ds(pl.multiple_of(first, block_rows), block_rows)

    def sum_copy(a, i):
        part, side = part_out.at[a], side_in.at[a]
        src, dst, to = (
            lambda: (part.at[slab(x + 2), low], far_in.at[a, 0], right),
            lambda: (part.at[slab(x + 2), high], far_in.at[a, 1], left),
            lambda: (part.at[slab(x + 1), high], side.at[0, :, high], right),
            lambda: (part.at[slab(x + 3), low], side.at[1, :, low], left),
            lambda: (both_out.at[a, 0], side.at[0, :, low], right),
            lambda: (both_out.at[a, 1], side.at[1, :, high], left),
            lambda: (pair_out.at[a], pair_in.at[a], at_tp(tp_of(x, 1 - z_hi))),
        )[i]()
        return remote(src, dst, sum_base[a] + i, to)

    def sum_start(a):
        for i in range(4):
            sum_copy(a, i).start()

    def sum_add(a):
        for i, (ring, columns) in enumerate(((x + 1, low), (x + 3, high))):
            sum_copy(a, i).wait_recv()
            own = part_out[a, slab(ring), columns].astype(F32)
            both_out[a, i] = (own + far_in[a, i].astype(F32)).astype(BF16)
            sum_copy(a, 4 + i).start()

    def sum_of_pair(a, pair):
        total = part_out[a, of_both(pair)].astype(F32)
        return total + sum(side_in[a, i, of_pair(pair)].astype(F32) for i in range(2))

    def sum_swap(a):
        for i in range(2, 6):
            sum_copy(a, i).wait_recv()
        pair_out[a] = sum_of_pair(a, 1 - z_hi).astype(BF16)
        sum_copy(a, 6).start()

    gather_key = [
        RingGather(sems, x, z_hi, functools.partial(own_block, key_in, a), tp_device)
        for a in range(2)
    ]

    def sum_end(a):
        total = own_rows[halves[a]] + sum_of_pair(a, z_hi)
        sum_copy(a, 6).wait_recv()
        encoded = (total + pair_in[a].astype(F32)).astype(BF16).astype(F32)
        key_in[a, mine] = norm_rows(encoded).astype(BF16)
        gather_key[a].start()

    kv_width = w_k.shape[1]
    own = seq_of(y, z_lo, core)

    def kv_block(a, ring, pair, which):
        return kv.at[seq_of(ring, pair, which), a]

    def kv_gather(a):
        return RingGather(
            sems, y, z_lo, lambda ring, pair: kv_block(a, ring, pair, core), seq_device
        )

    gather_kv = [kv_gather(a) for a in range(2)]
    share_kv = [
        CoreShare(sems, functools.partial(kv_block, a), core, other_core) for a in range(2)
    ]

    def to_kv(a):
        kv[own, a, :, :kv_width] = dot(key_in[a], w_k[...]).astype(BF16)
        kv[own, a, :, kv_width:] = dot(key_in[a], w_v[...]).astype(BF16)
        gather_kv[a].start()
        share_kv[a].send(0, y, z_lo)

    def kv_partner(a):
        gather_kv[a].partner()
        share_kv[a].send(1, y, 1 - z_lo)

    def kv_sides(a):
        gather_kv[a].sides()
        share_kv[a].send(2, y + 3, z_lo)
        share_kv[a].send(3, y + 1, z_lo)

    def kv_partner_sides(a):
        gather_kv[a].partner_sides()
        share_kv[a].send(4, y + 3, 1 - z_lo)
        share_kv[a].send(5, y + 1, 1 - z_lo)

    def kv_far(a):
        gather_kv[a].far()
        share_kv[a].send(6, y + 2, z_lo)

    def kv_partner_far(a):
        gather_kv[a].partner_far()
        share_kv[a].send(7, y + 2, 1 - z_lo)

    ones = jnp.ones((group, HEAD_DIM), BF16)

    def attend(here, a, blocks):
        for h in range(2):
            cols = slice(h * HEAD_DIM, (h + 1) * HEAD_DIM)
            v_cols = slice(kv_width + h * HEAD_DIM, kv_width + (h + 1) * HEAD_DIM)
            keys = jnp.concatenate([kv[b, a, :, cols] for b in blocks], axis=0)
            values = jnp.concatenate(
                [jnp.concatenate([kv[b, a, :, v_cols], ones], axis=1) for b in blocks], axis=0
            )
            scores = dot_t(q_ref[here, cols], keys)
            old = top_ref[h, here]
            new = jnp.maximum(old, jnp.max(scores, axis=1, keepdims=True))
            shrink = jnp.exp2(old - new)
            spread = jnp.concatenate([new] * (scores.shape[1] // HEAD_DIM), axis=1)
            weights = jnp.exp2(scores - spread)
            top_ref[h, here] = new
            acc_ref[h, here] = acc_ref[h, here] * jnp.concatenate([shrink] * 2, axis=1) + dot(
                weights.astype(BF16), values
            )

    pairs = (
        ((y, z_lo), (y, 1 - z_lo)),
        ((y + 3, z_lo), (y + 1, z_lo)),
        ((y + 3, 1 - z_lo), (y + 1, 1 - z_lo)),
        ((y + 2, z_lo), (y + 2, 1 - z_lo)),
    )

    def blocks_of(step):
        places = pairs[2 * step] + pairs[2 * step + 1]
        return [seq_of(*place, c) for place in places for c in (core, 1 - core)]

    def share_wait(a, step):
        for i in range(4):
            share_kv[a].wait(4 * step + i, *pairs[2 * step + i // 2][i % 2])

    def attend_all(a, step):
        share_wait(a, step)
        blocks = blocks_of(step)

        @pl.loop(0, rows // 512)
        def _(c):
            attend(pl.ds(pl.multiple_of(c * 512, 512), 512), a, blocks)

    make_queries(4, 6)
    w_start()
    gather_in[0].partner()
    gather_in[0].sides()
    gather_in[0].far()
    gather_in[1].partner()
    gather_in[1].sides()
    gather_in[1].far()
    gather_in[0].partner_sides()
    got_in.wait()
    gather_in[0].partner_far()
    to_hidden(0)
    got_out.wait()
    to_part(0)
    sum_start(0)
    gather_in[1].partner_sides()
    gather_in[1].partner_far()
    to_hidden(1)
    to_part(1)
    sum_add(0)
    sum_start(1)
    sum_swap(0)
    sum_add(1)
    sum_end(0)
    sum_swap(1)
    make_queries(6, 8)
    gather_key[0].partner()
    gather_key[0].sides()
    gather_key[0].far()
    sum_end(1)
    gather_key[0].partner_sides()
    got_k.wait()
    got_v.wait()
    gather_key[0].partner_far()
    to_kv(0)
    gather_key[1].partner()
    gather_key[1].sides()
    gather_key[1].far()
    kv_partner(0)
    kv_sides(0)
    kv_far(0)
    gather_key[1].partner_sides()
    gather_key[1].partner_far()
    to_kv(1)
    top_ref[...] = jnp.full(top_ref.shape, -1e30, F32)
    acc_ref[...] = jnp.zeros(acc_ref.shape, F32)
    kv_partner_sides(0)
    kv_partner_far(0)
    attend_all(0, 0)
    kv_partner(1)
    kv_sides(1)
    kv_far(1)
    w_sides()
    attend_all(0, 1)
    kv_partner_sides(1)
    kv_partner_far(1)
    attend_all(1, 0)
    share_wait(1, 1)

    att_base = sems.take(8)
    last_blocks = blocks_of(1)

    def att_copy(i, b, to, source, of):
        return pltpu.make_async_remote_copy(
            src_ref=att_out.at[to],
            dst_ref=att_in.at[source],
            send_sem=send_sem.at[att_base + i * 2 + b],
            recv_sem=recv_sem.at[att_base + i * 2 + of],
            device_id=at_tp(to),
            device_id_type=MESH,
        )

    @pl.loop(0, 4)
    def _(i):
        ring = (x + 1 + i) % 4
        here = pl.ds(pl.multiple_of(ring * 256, 256), 256)
        attend(here, 1, last_blocks)
        for h in range(2):
            done = acc_ref[h, here]
            done = (done[:, :HEAD_DIM] / done[:, HEAD_DIM:]).astype(BF16)
            cols = slice(h * HEAD_DIM, (h + 1) * HEAD_DIM)
            att_out[pl.ds(tp_of(ring, 0), 2), :, cols] = done.reshape(2, 128, HEAD_DIM)

        @pl.when(i < 3)
        def _():
            for b in range(2):
                att_copy(i, b, tp_of(ring, b), tp, z_hi).start()

    to_pair = tp_of(x, 1 - z_hi)
    att_copy(3, 0, to_pair, tp, 0).start()
    att_in[pl.ds(tp, 1)] = att_out[pl.ds(tp, 1)]

    w_far()

    @pl.loop(0, 3)
    def _(i):
        for b in range(2):
            to = tp_of(x + 1 + i, b)
            source = tp_of(x + 3 - i, b)
            copy = att_copy(i, b, to, source, b)
            copy.wait_send()
            copy.wait_recv()

    att_copy(3, 0, to_pair, to_pair, 0).wait()

    @pl.loop(0, width // 256)
    def _(c):
        here = pl.ds(pl.multiple_of(c * 256, 256), 256)
        total = dot(att_in[0], w_p[0, 0, :, here])
        for t in range(1, N_TP):
            total = total + dot(att_in[t], w_p[t % 2, t // 2, :, here])
        proj[:, here] = total

    normal = norm_rows(proj[...])
    part = width // N_TP
    res_base = sems.take(N_TP)
    for t in range(N_TP):
        columns = normal[:, t * part : (t + 1) * part]
        half_rows = columns.shape[0] // 2
        sides = jnp.concatenate([columns[:half_rows], columns[half_rows:]], axis=1)
        res_out[t] = sides.astype(BF16)

    def res_copy(d, source):
        to = (tp + d) % N_TP
        return remote(res_out.at[to], out_ref.at[source], res_base + d, at_tp(to))

    @pl.loop(1, N_TP)
    def _(d):
        res_copy(d, tp).start()

    keep = pltpu.make_async_copy(res_out.at[tp], out_ref.at[tp], local_sem.at[7])
    keep.start()

    @pl.loop(1, N_TP)
    def _(d):
        res_copy(d, (tp + N_TP - d) % N_TP).wait()

    keep.wait()
    assert sems.used <= 160
    for transfer in (*gather_in, *gather_key, *gather_kv, *share_kv):
        transfer.drain()
    for a in range(2):
        for i in range(7):
            sum_copy(a, i).wait_send()
    w_drain()


def add_kernel(tok_ref, normal_ref, out_ref):
    rows, part = out_ref.shape
    which = lax.axis_index("tp") % 2
    own = jnp.where(which == 0, tok_ref[:, :part].astype(F32), tok_ref[:, part:].astype(F32))
    normal = normal_ref[...].astype(F32)
    normal = jnp.concatenate([normal[:, :, :part], normal[:, :, part:]], axis=1)
    out_ref[...] = own + normal.reshape(rows, part)


def shards(tokens, visible, w_in, w_out, w_query, w_key, w_value, w_proj):
    rows, width = tokens.shape
    part = width // N_TP
    block_rows = rows // 64
    group = block_rows * N_TP
    any_spec = pl.BlockSpec(memory_space=pl.ANY)
    vmem_spec = pl.BlockSpec(memory_space=pltpu.VMEM)
    heads = w_query.shape[1]
    result = pl.pallas_call(
        kernel,
        out_shape=jax.ShapeDtypeStruct((N_TP, rows // N_TP // 2, 2 * part), BF16),
        in_specs=[vmem_spec] * 2 + [any_spec] * 7,
        out_specs=any_spec,
        scratch_shapes=[
            pltpu.VMEM(tokens.shape, BF16),
            pltpu.VMEM(w_in.shape, BF16),
            pltpu.VMEM(w_out.shape, BF16),
            pltpu.VMEM(w_query.shape, BF16),
            pltpu.VMEM(w_key.shape, BF16),
            pltpu.VMEM(w_value.shape, BF16),
            pltpu.VMEM((2, 4, *w_proj.shape), BF16),
            pltpu.VMEM((N_SEQ, 8, rows // 8), jnp.int32),
            pltpu.VMEM((16 * N_SEQ, width // 2), BF16),
            pltpu.VMEM((16 * N_SEQ, width // 2), BF16),
            pltpu.VMEM((2 * block_rows, width), F32),
            pltpu.VMEM((2, group, width), BF16),
            pltpu.VMEM((2, group, w_in.shape[1]), BF16),
            pltpu.VMEM((2, group, width), BF16),
            pltpu.VMEM((2, 2, 2 * block_rows, width // 2), BF16),
            pltpu.VMEM((2, 2, 2 * block_rows, width // 2), BF16),
            pltpu.VMEM((2, 2, 2 * block_rows, width), BF16),
            pltpu.VMEM((2, block_rows, width), BF16),
            pltpu.VMEM((2, block_rows, width), BF16),
            pltpu.VMEM((2, group, width), BF16),
            pltpu.VMEM((N_SEQ, 2, group, 2 * heads), BF16),
            pltpu.VMEM((rows, heads), BF16),
            pltpu.VMEM((2, rows, HEAD_DIM), F32),
            pltpu.VMEM((2, rows, 2 * HEAD_DIM), F32),
            pltpu.VMEM((N_TP, rows // N_TP, heads), BF16),
            pltpu.VMEM((N_TP, rows // N_TP, heads), BF16),
            pltpu.VMEM((rows // N_TP, width), F32),
            pltpu.VMEM((N_TP, rows // N_TP // 2, 2 * part), BF16),
            pltpu.SemaphoreType.DMA((8,)),
            pltpu.SemaphoreType.DMA((160,)),
            pltpu.SemaphoreType.DMA((160,)),
        ],
        compiler_params=pltpu.CompilerParams(
            collective_id=0, has_side_effects=True, vmem_limit_bytes=60 * 1024 * 1024
        ),
        name="generator_step",
    )(
        visible.reshape(8, rows // 8),
        visible.reshape(1, rows),
        tokens,
        w_in,
        w_out,
        w_query,
        w_key,
        w_value,
        w_proj,
    )
    tile = rows // 4
    return pl.pallas_call(
        add_kernel,
        grid=(rows // tile,),
        out_shape=jax.ShapeDtypeStruct((rows, part), F32),
        in_specs=[
            pl.BlockSpec((tile, 2 * part), lambda i: (i, lax.axis_index("tp") // 2)),
            pl.BlockSpec((N_TP // 4, rows // N_TP // 2, 2 * part), lambda i: (i, 0, 0)),
        ],
        out_specs=pl.BlockSpec((tile, part), lambda i: (i, 0)),
        name="residual",
    )(tokens, result)


def solution(mesh):
    in_specs = (
        P("seq", None),
        P("seq"),
        P(None, "tp"),
        P("tp", None),
        P(None, "tp"),
        P(None, "tp"),
        P(None, "tp"),
        P("tp", None),
    )
    out_specs = P("seq", "tp")
    return jax.shard_map(shards, mesh=mesh, in_specs=in_specs, out_specs=out_specs, check_vma=False)
```

time: 145 us -> 127 us (0.88)
  Pallas kernels: 137 us -> 122 us
  other arithmetic: 3.8 us -> 0 us
    pallas_call x1, Pallas kernels: 137 us -> 118 us  [shards(): pl.pallas_call(kernel, out_shape=jax.ShapeDtypeStruct((N_TP, rows // N_TP...]
    pallas_call x0 -> x1, Pallas kernels: none -> 3.92 us  [shards(): pl.pallas_call(add_kernel, grid=(rows // tile,), out_shape=jax.ShapeDtype...]
    pallas_call x0 -> x1, local copies, waits for them, and re-layouts: none -> 2.92 us  [shards(): pl.pallas_call(add_kernel, grid=(rows // tile,), out_shape=jax.ShapeDtype...]
    convert_element_type x2 -> x0, other arithmetic: 2.52 us -> none  [the longest x1 1.28 us: shards(): visible = (visible > 0).astype(jnp.int32)]
    dynamic_slice x1 -> x0, local copies, waits for them, and re-layouts: 1.58 us -> none  [shards(): own_cols = lax.dynamic_slice_in_dim(tokens, tp_index * part, part, 1)]
where the time goes in v2:
time: 127 us; the launch traced here: 125 us
  Pallas kernels  122 us (96%)
  local copies, waits for them, and re-layouts  2.92 us (2%)
    pallas_call x1, Pallas kernels, shards(): pl.pallas_call(kernel, out_shape=jax.ShapeDtypeStruct((N_TP, rows // N_TP...  118 us
    pallas_call x1, Pallas kernels, shards(): pl.pallas_call(add_kernel, grid=(rows // tile,), out_shape=jax.ShapeDtype...  3.92 us
    pallas_call x1, local copies, waits for them, and re-layouts, shards(): pl.pallas_call(add_kernel, grid=(rows // tile,), out_shape=jax.ShapeDtype...  2.92 us

profile of v2, /device:TPU:0, one launch (start us, length us, event | category | flops | bytes accessed | tf_op | source)
XLA Modules:
  0.0 124.8 jit_solution(15738935218245266152)
XLA Ops:
  0.0 118.0 %generator_step.1.normal_ref = bf16[8,64,640]{2,1,0:T(8,128)(2,1)} custom-call(s32[8,128]{1,0:T(8,128)} %bitcast.2, s32[1,1024]{1,0:T(1,128)} %bitcast.3, bf16[1024,2560]{1,0:T(8,128)(2,1)} %tok_ref.1, bf16[2560,1280]{1,0:T(8,128)(2,1)} %w_in_hbm.1, bf16[1280,2560]{1,0:T(8,128)(2,1)} %w_out_hbm.1, bf16[2560,256]{1,0:T(8,128)(2,1)} %w_q_hbm.1, ...), custom_call_target="tpu_custom_call" | custom-call | tf_op jit(solution)/shard_map/generator_step/pallas_call | solution.py:760
  118.0 3.9 %residual.1 = f32[1024,320]{1,0:T(8,128)} custom-call(bf16[1024,2560]{1,0:T(8,128)(2,1)} %tok_ref.1, bf16[8,64,640]{2,1,0:T(8,128)(2,1)} %generator_step.1.normal_ref), custom_call_target="tpu_custom_call" | custom-call | tf_op jit(solution)/shard_map/residual/pallas_call | solution.py:814
  121.9 2.9 %copy.9 = f32[1024,320]{0,1:T(8,128)} copy(f32[1024,320]{1,0:T(8,128)} %residual.1) | data formatting | bytes 2621440 | tf_op jit(solution)/shard_map/residual/pallas_call | solution.py:814

commit v3 on v2

--- a/solution.py
+++ b/solution.py
@@ -43,14 +43,16 @@
 
 
 class RingGather:
-    def __init__(self, sems, ring, pair, block, device):
-        self.sems, self.ring, self.pair = sems, ring, pair
+    def __init__(self, sems, ring, pair, block, device, half=None):
+        self.sems, self.ring, self.pair, self.half = sems, ring, pair, half
         self.block, self.device = block, device
-        self.base = sems.take(7)
+        self.base = sems.take(8)
         self.sent = []
 
     def _copy(self, i, ring, pair, device):
         ref = self.block(ring, pair)
+        if self.half is not None and i in (3, 7):
+            ref = self.half(ref, i // 7)
         return pltpu.make_async_remote_copy(
             src_ref=ref,
             dst_ref=ref,
@@ -73,7 +75,8 @@
         self._send(0, r, p, r, 1 - p)
         self._send(1, r, p, r + 1, p)
         self._send(2, r, p, r + 3, p)
-        self._send(3, r, p, r + 2, p)
+        if self.half is None:
+            self._send(3, r, p, r + 2, p)
 
     def partner(self):
         r, p = self.ring, self.pair
@@ -82,12 +85,19 @@
         self._send(5, r, 1 - p, r + 3, p)
 
     def sides(self):
-        self._wait(1, self.ring + 3, self.pair)
-        self._wait(2, self.ring + 1, self.pair)
+        r, p = self.ring, self.pair
+        self._wait(1, r + 3, p)
+        if self.half is not None:
+            self._send(3, r + 3, p, r + 1, p)
+        self._wait(2, r + 1, p)
+        if self.half is not None:
+            self._send(7, r + 1, p, r + 3, p)
 
     def far(self):
         r, p = self.ring, self.pair
         self._wait(3, r + 2, p)
+        if self.half is not None:
+            self._wait(7, r + 2, p)
         self._send(6, r + 2, p, r, 1 - p)
 
     def partner_sides(self):
@@ -171,6 +181,11 @@
     att_in,
     proj,
     res_out,
+    res_in,
+    stat_out,
+    stat_in,
+    own_cols,
+    result,
     local_sem,
     send_sem,
     recv_sem,
@@ -473,7 +488,11 @@
         return remote(src, dst, sum_base[a] + i, to)
 
     def sum_start(a):
-        for i in range(4):
+        for i in range(2):
+            sum_copy(a, i).start()
+
+    def sum_sides(a):
+        for i in range(2, 4):
             sum_copy(a, i).start()
 
     def sum_add(a):
@@ -511,9 +530,17 @@
     def kv_block(a, ring, pair, which):
         return kv.at[seq_of(ring, pair, which), a]
 
+    def half_of(ref, half):
+        return ref.at[pl.ds(half * (group // 2), group // 2)]
+
     def kv_gather(a):
         return RingGather(
-            sems, y, z_lo, lambda ring, pair: kv_block(a, ring, pair, core), seq_device
+            sems,
+            y,
+            z_lo,
+            lambda ring, pair: kv_block(a, ring, pair, core),
+            seq_device,
+            half=half_of if a == 0 else None,
         )
 
     gather_kv = [kv_gather(a) for a in range(2)]
@@ -593,6 +620,17 @@
         def _(c):
             attend(pl.ds(pl.multiple_of(c * 512, 512), 512), a, blocks)
 
+
+    def transpose_own():
+        part = width // N_TP
+        both_cols = pl.ds(pl.multiple_of(x * 2 * part, 2 * part), 2 * part)
+
+        @pl.loop(0, rows // 128)
+        def _(c):
+            here = pl.ds(pl.multiple_of(c * 128, 128), 128)
+            wide = tok[here, both_cols].astype(F32)
+            own_cols[:, here] = jnp.where(z_hi == 0, wide[:, :part], wide[:, part:]).T.astype(BF16)
+
     make_queries(4, 6)
     w_start()
     gather_in[0].partner()
@@ -611,14 +649,17 @@
     gather_in[1].partner_sides()
     gather_in[1].partner_far()
     to_hidden(1)
+    sum_sides(0)
     to_part(1)
     sum_add(0)
     sum_start(1)
     sum_swap(0)
+    sum_sides(1)
     sum_add(1)
     sum_end(0)
     sum_swap(1)
     make_queries(6, 8)
+    transpose_own()
     gather_key[0].partner()
     gather_key[0].sides()
     gather_key[0].far()
@@ -631,8 +672,8 @@
     gather_key[1].partner()
     gather_key[1].sides()
     gather_key[1].far()
+    kv_sides(0)
     kv_partner(0)
-    kv_sides(0)
     kv_far(0)
     gather_key[1].partner_sides()
     gather_key[1].partner_far()
@@ -698,55 +739,95 @@
 
     att_copy(3, 0, to_pair, to_pair, 0).wait()
 
-    @pl.loop(0, width // 256)
-    def _(c):
-        here = pl.ds(pl.multiple_of(c * 256, 256), 256)
+    part = width // N_TP
+    res_base = sems.take(8)
+    stat_base = sems.take(N_TP)
+
+    def res_copy(i, b, to, source, of):
+        return pltpu.make_async_remote_copy(
+            src_ref=res_out.at[to],
+            dst_ref=res_in.at[source],
+            send_sem=send_sem.at[res_base + i * 2 + b],
+            recv_sem=recv_sem.at[res_base + i * 2 + of],
+            device_id=at_tp(to),
+            device_id_type=MESH,
+        )
+
+    @pl.loop(0, 4)
+    def _(i):
+        ring = (x + 1 + i) % 4
+        here = pl.ds(pl.multiple_of(ring * 2 * part, 2 * part), 2 * part)
         total = dot(att_in[0], w_p[0, 0, :, here])
         for t in range(1, N_TP):
             total = total + dot(att_in[t], w_p[t % 2, t // 2, :, here])
         proj[:, here] = total
-
-    normal = norm_rows(proj[...])
-    part = width // N_TP
-    res_base = sems.take(N_TP)
-    for t in range(N_TP):
-        columns = normal[:, t * part : (t + 1) * part]
-        half_rows = columns.shape[0] // 2
-        sides = jnp.concatenate([columns[:half_rows], columns[half_rows:]], axis=1)
-        res_out[t] = sides.astype(BF16)
-
-    def res_copy(d, source):
-        to = (tp + d) % N_TP
-        return remote(res_out.at[to], out_ref.at[source], res_base + d, at_tp(to))
+        for b in range(2):
+            block = total[:, b * part : (b + 1) * part].T.astype(BF16)
+            res_out[pl.ds(tp_of(ring, b), 1)] = block[None]
+
+        @pl.when(i < 3)
+        def _():
+            for b in range(2):
+                res_copy(i, b, tp_of(ring, b), tp, z_hi).start()
+
+    res_copy(3, 0, to_pair, tp, 0).start()
+    res_in[pl.ds(tp, 1)] = res_out[pl.ds(tp, 1)]
+    row_mean = jnp.mean(proj[...], axis=1, keepdims=True)
+    centred = proj[...] - row_mean
+    scale = lax.rsqrt(jnp.mean(centred * centred, axis=1, keepdims=True) + EPSILON)
+    lane = lax.broadcasted_iota(jnp.int32, (HEAD_DIM, HEAD_DIM), 1)
+    stat_out[...] = jnp.where(lane == 0, row_mean, scale).T[:8]
+
+    def stat_copy(d, source):
+        return remote(stat_out, stat_in.at[source], stat_base + d, at_tp((tp + d) % N_TP))
 
     @pl.loop(1, N_TP)
     def _(d):
-        res_copy(d, tp).start()
-
-    keep = pltpu.make_async_copy(res_out.at[tp], out_ref.at[tp], local_sem.at[7])
-    keep.start()
+        stat_copy(d, tp).start()
+
+    stat_in[pl.ds(tp, 1)] = stat_out[...][None]
+
+    def finish(source):
+        here = pl.ds(pl.multiple_of(source * HEAD_DIM, HEAD_DIM), HEAD_DIM)
+        stats = stat_in[source]
+        normal = (res_in[source].astype(F32) - stats[:1]) * stats[1:2]
+        result[:, here] = own_cols[:, here].astype(F32) + normal
+        copy = pltpu.make_async_copy(
+            result.at[:, here], out_ref.at[:, here], local_sem.at[8 + source]
+        )
+        copy.start()
+
+    finish(tp)
 
     @pl.loop(1, N_TP)
     def _(d):
-        res_copy(d, (tp + N_TP - d) % N_TP).wait()
-
-    keep.wait()
-    assert sems.used <= 160
+        stat_copy(d, (tp + N_TP - d) % N_TP).wait()
+
+    res_copy(3, 0, to_pair, to_pair, 0).wait()
+    finish(to_pair)
+
+    @pl.loop(0, 3)
+    def _(i):
+        for b in range(2):
+            source = tp_of(x + 3 - i, b)
+            copy = res_copy(i, b, tp_of(x + 1 + i, b), source, b)
+            copy.wait_send()
+            copy.wait_recv()
+            finish(source)
+
+    @pl.loop(0, N_TP)
+    def _(t):
+        here = pl.ds(pl.multiple_of(t * HEAD_DIM, HEAD_DIM), HEAD_DIM)
+        pltpu.make_async_copy(
+            result.at[:, here], out_ref.at[:, here], local_sem.at[8 + t]
+        ).wait()
+
     for transfer in (*gather_in, *gather_key, *gather_kv, *share_kv):
         transfer.drain()
     for a in range(2):
         for i in range(7):
             sum_copy(a, i).wait_send()
     w_drain()
-
-
-def add_kernel(tok_ref, normal_ref, out_ref):
-    rows, part = out_ref.shape
-    which = lax.axis_index("tp") % 2
-    own = jnp.where(which == 0, tok_ref[:, :part].astype(F32), tok_ref[:, part:].astype(F32))
-    normal = normal_ref[...].astype(F32)
-    normal = jnp.concatenate([normal[:, :, :part], normal[:, :, part:]], axis=1)
-    out_ref[...] = own + normal.reshape(rows, part)
 
 
 def shards(tokens, visible, w_in, w_out, w_query, w_key, w_value, w_proj):
@@ -759,7 +840,7 @@
     heads = w_query.shape[1]
     result = pl.pallas_call(
         kernel,
-        out_shape=jax.ShapeDtypeStruct((N_TP, rows // N_TP // 2, 2 * part), BF16),
+        out_shape=jax.ShapeDtypeStruct((part, rows), F32),
         in_specs=[vmem_spec] * 2 + [any_spec] * 7,
         out_specs=any_spec,
         scratch_shapes=[
@@ -790,8 +871,13 @@
             pltpu.VMEM((N_TP, rows // N_TP, heads), BF16),
             pltpu.VMEM((N_TP, rows // N_TP, heads), BF16),
             pltpu.VMEM((rows // N_TP, width), F32),
-            pltpu.VMEM((N_TP, rows // N_TP // 2, 2 * part), BF16),
-            pltpu.SemaphoreType.DMA((8,)),
+            pltpu.VMEM((N_TP, part, rows // N_TP), BF16),
+            pltpu.VMEM((N_TP, part, rows // N_TP), BF16),
+            pltpu.VMEM((8, rows // N_TP), F32),
+            pltpu.VMEM((N_TP, 8, rows // N_TP), F32),
+            pltpu.VMEM((part, rows), BF16),
+            pltpu.VMEM((part, rows), F32),
+            pltpu.SemaphoreType.DMA((16,)),
             pltpu.SemaphoreType.DMA((160,)),
             pltpu.SemaphoreType.DMA((160,)),
         ],
@@ -810,18 +896,7 @@
         w_value,
         w_proj,
     )
-    tile = rows // 4
-    return pl.pallas_call(
-        add_kernel,
-        grid=(rows // tile,),
-        out_shape=jax.ShapeDtypeStruct((rows, part), F32),
-        in_specs=[
-            pl.BlockSpec((tile, 2 * part), lambda i: (i, lax.axis_index("tp") // 2)),
-            pl.BlockSpec((N_TP // 4, rows // N_TP // 2, 2 * part), lambda i: (i, 0, 0)),
-        ],
-        out_specs=pl.BlockSpec((tile, part), lambda i: (i, 0)),
-        name="residual",
-    )(tokens, result)
+    return result.T
 
 
 def solution(mesh):

time: 127 us -> 121 us (0.953); the launches traced: 125 us -> 120 us
  Pallas kernels: 122 us -> 118 us
    pallas_call x2 -> x1, Pallas kernels: 122 us -> 118 us  [shards(): pl.pallas_call(kernel, out_shape=jax.ShapeDtypeStruct((part, rows), F32),...]
    pallas_call x1 -> x0, local copies, waits for them, and re-layouts: 2.92 us -> none  [shards(): pl.pallas_call(add_kernel, grid=(rows // tile,), out_shape=jax.ShapeDtype...]
    unnamed x0 -> x1, local copies, waits for them, and re-layouts: none -> 2.52 us
where the time goes in v3:
time: 121 us; the launch traced here: 120 us
  Pallas kernels  118 us (98%)
  local copies, waits for them, and re-layouts  2.52 us (2%)
    pallas_call x1, Pallas kernels, shards(): pl.pallas_call(kernel, out_shape=jax.ShapeDtypeStruct((part, rows), F32),...  118 us
    unnamed x1, local copies, waits for them, and re-layouts  2.52 us

profile of v3, /device:TPU:0, one launch (start us, length us, event | category | flops | bytes accessed | tf_op | source)
XLA Modules:
  0.0 120.2 jit_solution(5651558601538665868)
XLA Ops:
  0.0 117.7 %generator_step.1 = f32[320,1024]{1,0:T(8,128)} custom-call(s32[8,128]{1,0:T(8,128)} %bitcast.4, s32[1,1024]{1,0:T(1,128)} %bitcast.5, bf16[1024,2560]{1,0:T(8,128)(2,1)} %tok_hbm.1, bf16[2560,1280]{1,0:T(8,128)(2,1)} %w_in_hbm.1, bf16[1280,2560]{1,0:T(8,128)(2,1)} %w_out_hbm.1, bf16[2560,256]{1,0:T(8,128)(2,1)} %w_q_hbm.1, bf16[2560,256]{1,0:T(8,128)(2,1)} %w_k_hbm.1, ...), custom_call_target="tpu_custom_call" | custom-call | tf_op jit(solution)/shard_map/generator_step/pallas_call | solution.py:841
  117.7 2.5 %copy.10 = f32[1024,320]{0,1:T(8,128)} copy(f32[1024,320]{0,1:T(8,128)} %bitcast.3) | data formatting | bytes 2621440

commit v4 on v3

--- a/solution.py
+++ b/solution.py
@@ -397,21 +397,24 @@
         )
         gather_in[a].start()
 
-    def w_block(ring, which, half=None):
-        if half is None:
-            return w_p.at[:, :, slice_of(ring, which)]
-        return w_p.at[half, :, slice_of(ring, which)]
-
     def seq_device(ring, pair):
         return at_seq(seq_of(ring, pair, core))
 
     other_core = at_seq(seq_of(y, z_lo, 1 - core))
     up, down = seq_device(y + 1, z_lo), seq_device(y + 3, z_lo)
-    w_base = sems.take(8)
-
-    def w_copy(i, ring, which=None, half=None):
-        ref = w_block(ring, core if which is None else which, half)
-        return remote(ref, ref, w_base + i, (up, down, up, down)[i] if i < 4 else other_core)
+    w_base = sems.take(11)
+
+    def w_copy(i, ring, which=None):
+        ref = w_p.at[:, :, slice_of(ring, core if which is None else which)]
+        return remote(ref, ref, w_base + i, (up, down)[i] if i < 2 else other_core)
+
+    def w_part(i, ring):
+        ref = w_p.at[i, x, slice_of(ring, core)]
+        return remote(ref, ref, w_base + 2 + i, (up, down)[i])
+
+    def w_cross(d, block):
+        ref = w_p.at[:, block, slice_of(y + 2, core)]
+        return remote(ref, ref, w_base + 7 + d, at_tp(tp_of(x + d, z_hi)))
 
     def w_start():
         got_p.wait()
@@ -430,22 +433,38 @@
 
     def w_sides():
         w_copy(0, y + 3).wait_recv()
-        w_copy(2, y + 3, half=0).start()
+        w_part(0, y + 3).start()
         w_copy(5, y + 3).start()
         w_copy(1, y + 1).wait_recv()
-        w_copy(3, y + 1, half=1).start()
+        w_part(1, y + 1).start()
         w_copy(6, y + 1).start()
 
+    def w_spread():
+        w_part(0, y + 2).wait_recv()
+        w_part(1, y + 2).wait_recv()
+
+        @pl.loop(1, 4)
+        def _(d):
+            w_cross(d, x).start()
+
     def w_far():
-        w_copy(2, y + 2, half=0).wait_recv()
-        w_copy(3, y + 2, half=1).wait_recv()
+        @pl.loop(1, 4)
+        def _(d):
+            w_cross(d, (x + 4 - d) % 4).wait_recv()
+
         w_copy(7, y + 2).start()
         for i, ring in enumerate((y, y + 3, y + 1, y + 2)):
             w_copy(4 + i, ring, 1 - core).wait_recv()
 
     def w_drain():
-        for i, ring in enumerate((y, y, y + 3, y + 1, y, y + 3, y + 1, y + 2)):
-            w_copy(i, ring, half=(None, None, 0, 1)[i] if i < 4 else None).wait_send()
+        for i, ring in ((0, y), (1, y), (4, y), (5, y + 3), (6, y + 1), (7, y + 2)):
+            w_copy(i, ring).wait_send()
+        w_part(0, y + 3).wait_send()
+        w_part(1, y + 1).wait_send()
+
+        @pl.loop(1, 4)
+        def _(d):
+            w_cross(d, x).wait_send()
 
     def to_hidden(a):
         @pl.loop(0, hidden.shape[2] // 256)
@@ -664,6 +683,7 @@
     gather_key[0].sides()
     gather_key[0].far()
     sum_end(1)
+    w_sides()
     gather_key[0].partner_sides()
     got_k.wait()
     got_v.wait()
@@ -678,6 +698,7 @@
     gather_key[1].partner_sides()
     gather_key[1].partner_far()
     to_kv(1)
+    w_spread()
     top_ref[...] = jnp.full(top_ref.shape, -1e30, F32)
     acc_ref[...] = jnp.zeros(acc_ref.shape, F32)
     kv_partner_sides(0)
@@ -686,7 +707,6 @@
     kv_partner(1)
     kv_sides(1)
     kv_far(1)
-    w_sides()
     attend_all(0, 1)
     kv_partner_sides(1)
     kv_partner_far(1)

time: 121 us -> 119 us (0.983)
  Pallas kernels: 118 us -> 116 us
    pallas_call x1, Pallas kernels: 118 us -> 116 us  [shards(): pl.pallas_call(kernel, out_shape=jax.ShapeDtypeStruct((part, rows), F32),...]
where the time goes in v4:
time: 119 us
  Pallas kernels  116 us (97%)
  local copies, waits for them, and re-layouts  2.52 us (2%)
    pallas_call x1, Pallas kernels, shards(): pl.pallas_call(kernel, out_shape=jax.ShapeDtypeStruct((part, rows), F32),...  116 us
    unnamed x1, local copies, waits for them, and re-layouts  2.52 us

profile of v4, /device:TPU:0, one launch (start us, length us, event | category | flops | bytes accessed | tf_op | source)
XLA Modules:
  0.0 118.8 jit_solution(8762158658239598314)
XLA Ops:
  0.0 116.3 %generator_step.1 = f32[320,1024]{1,0:T(8,128)} custom-call(s32[8,128]{1,0:T(8,128)} %bitcast.4, s32[1,1024]{1,0:T(1,128)} %bitcast.5, bf16[1024,2560]{1,0:T(8,128)(2,1)} %tok_hbm.1, bf16[2560,1280]{1,0:T(8,128)(2,1)} %w_in_hbm.1, bf16[1280,2560]{1,0:T(8,128)(2,1)} %w_out_hbm.1, bf16[2560,256]{1,0:T(8,128)(2,1)} %w_q_hbm.1, bf16[2560,256]{1,0:T(8,128)(2,1)} %w_k_hbm.1, ...), custom_call_target="tpu_custom_call" | custom-call | tf_op jit(solution)/shard_map/generator_step/pallas_call | solution.py:861
  116.3 2.5 %copy.10 = f32[1024,320]{0,1:T(8,128)} copy(f32[1024,320]{0,1:T(8,128)} %bitcast.3) | data formatting | bytes 2621440

commit v5 on v4

--- a/solution.py
+++ b/solution.py
@@ -271,8 +271,9 @@
 
     @pl.loop(1, N_SEQ)
     def _(d):
+        far_first = (d + 6) % (N_SEQ - 1) + 1
         remote(
-            vis_tile, counts.at[seq], count_base + d, at_seq((seq + d) % N_SEQ)
+            vis_tile, counts.at[seq], count_base + far_first, at_seq((seq + far_first) % N_SEQ)
         ).start()
 
     counts[pl.ds(seq, 1)] = vis_tile[...][None]
@@ -333,9 +334,10 @@
 
     @pl.loop(1, N_SEQ)
     def _(d):
-        to = (seq + d) % N_SEQ
+        far_first = (d + 6) % (N_SEQ - 1) + 1
+        to = (seq + far_first) % N_SEQ
         remote(
-            pick_out.at[pick_rows(to)], pick_in.at[pick_rows(seq)], pick_base + d, at_seq(to)
+            pick_out.at[pick_rows(to)], pick_in.at[pick_rows(seq)], pick_base + far_first, at_seq(to)
         ).start()
 
     pick_in[pick_rows(seq)] = pick_out[pick_rows(seq)]

time: 119 us -> 121 us (1.017)
  Pallas kernels: 116 us -> 118 us
    pallas_call x1, Pallas kernels: 116 us -> 118 us  [shards(): pl.pallas_call(kernel, out_shape=jax.ShapeDtypeStruct((part, rows), F32),...]
where the time goes in v5:
time: 121 us; the launch traced here: 120 us
  Pallas kernels  118 us (98%)
  local copies, waits for them, and re-layouts  2.52 us (2%)
    pallas_call x1, Pallas kernels, shards(): pl.pallas_call(kernel, out_shape=jax.ShapeDtypeStruct((part, rows), F32),...  118 us
    unnamed x1, local copies, waits for them, and re-layouts  2.52 us

profile of v5, /device:TPU:0, one launch (start us, length us, event | category | flops | bytes accessed | tf_op | source)
XLA Modules:
  0.0 120.4 jit_solution(11877832406312716648)
XLA Ops:
  0.0 117.9 %generator_step.1 = f32[320,1024]{1,0:T(8,128)} custom-call(s32[8,128]{1,0:T(8,128)} %bitcast.4, s32[1,1024]{1,0:T(1,128)} %bitcast.5, bf16[1024,2560]{1,0:T(8,128)(2,1)} %tok_hbm.1, bf16[2560,1280]{1,0:T(8,128)(2,1)} %w_in_hbm.1, bf16[1280,2560]{1,0:T(8,128)(2,1)} %w_out_hbm.1, bf16[2560,256]{1,0:T(8,128)(2,1)} %w_q_hbm.1, bf16[2560,256]{1,0:T(8,128)(2,1)} %w_k_hbm.1, ...), custom_call_target="tpu_custom_call" | custom-call | tf_op jit(solution)/shard_map/generator_step/pallas_call | solution.py:863
  117.9 2.5 %copy.10 = f32[1024,320]{0,1:T(8,128)} copy(f32[1024,320]{0,1:T(8,128)} %bitcast.3) | data formatting | bytes 2621440
